TPU v7x, 128 devices: a whole 4x4x4 slice. The times are simulated.
128 devices in a mesh: row: 16 (over z, x), col: 8 (over y, core).
Axes of the slice: x: 4, y: 4, z: 4, core: 2. Of those that a mesh axis runs over, the one named last changes fastest.
Arguments:
- right_side: float32 [64, 1024, 256], P('row', 'col'), may hold values from -12 to 12
- permeability: bfloat16 [64, 1024, 256], P('row', 'col'), may hold values from 0.25 to 4
- lift_weight: float32 [16, 3], replicated, may hold values from -3 to 3
- spectral_weight: float32 [2, 32, 16, 16, 512], P(None, 'row', None, None, 'col'), may hold values from -3 to 3
- mix_weight: float32 [16, 17], replicated, may hold values from -3 to 3
- proj_weight: float32 [17], replicated, may hold values from -3 to 3
Outputs:
- solution: float32 [64, 1024, 256], P('row', 'col')
- residual: float32 [64, 1024, 256], P('row', 'col')
- kept: float32 [2, 64, 1024, 256], P(None, 'row', 'col')
All inputs are finite; a program needn't handle non-finite values.
Results may differ from a plain program's by a relative error of at most 0.0007.
Values may be sent and summed in bfloat16 or wider, within the bound.
A program may use at most 128 MiB of HBM per device.

v0:
```python
import jax
import jax.numpy as jnp
from jax import lax
from jax.sharding import PartitionSpec as P

CHANNELS = 16
KX = 16
KY = 32
KZ = 32
ITERS = 2


HIGHEST = lax.Precision.HIGHEST


def with_halo(block, sides, width):
    for axis, dim in sides:
        count = lax.axis_size(axis)
        forward = [(i, i + 1) for i in range(count - 1)]
        backward = [(target, source) for source, target in forward]
        low = lax.ppermute(
            lax.slice_in_dim(block, block.shape[dim] - width, None, axis=dim), axis, forward
        )
        high = lax.ppermute(lax.slice_in_dim(block, 0, width, axis=dim), axis, backward)
        block = jnp.concatenate([low, block, high], axis=dim)
    return block


def einsum_high(form, left, right):
    return jnp.einsum(form, left, right, precision=HIGHEST)


def harmonic(first, second):
    return 2.0 * first * second / (first + second)


def wave_table(freqs, places, length):
    turns = freqs[None, :] * places[:, None] % length
    angle = turns.astype(jnp.float32) * (2.0 * jnp.pi / length)
    return (jnp.cos(angle), jnp.sin(angle))


def signed_freqs(count):
    return jnp.arange(count, dtype=jnp.int32) - count // 2


def face_arrays(permeability):
    padded = with_halo(permeability, (("row", 0), ("col", 1)), 1).astype(jnp.float32)
    own = permeability.astype(jnp.float32)
    edged = jnp.pad(own, ((1, 1), (1, 1), (0, 0)), mode="edge")
    padded = jnp.where(padded > 0.0, padded, edged)
    first = harmonic(padded[:-1, 1:-1], padded[1:, 1:-1])
    second = harmonic(padded[1:-1, :-1], padded[1:-1, 1:])
    deep = jnp.pad(own, ((0, 0), (0, 0), (1, 1)), mode="edge")
    third = harmonic(deep[:, :, :-1], deep[:, :, 1:])
    return ((first, second, third), jnp.log(own))


def apply_operator(field, faces):
    first, second, third = faces
    padded = with_halo(field, (("row", 0), ("col", 1)), 1)
    padded = jnp.pad(padded, ((0, 0), (0, 0), (1, 1)))
    total = first[:-1] * (field - padded[:-2, 1:-1, 1:-1])
    total = total + first[1:] * (field - padded[2:, 1:-1, 1:-1])
    total = total + second[:, :-1] * (field - padded[1:-1, :-2, 1:-1])
    total = total + second[:, 1:] * (field - padded[1:-1, 2:, 1:-1])
    total = total + third[:, :, :-1] * (field - padded[1:-1, 1:-1, :-2])
    total = total + third[:, :, 1:] * (field - padded[1:-1, 1:-1, 2:])
    return total


def global_squares(field):
    return lax.psum(jnp.sum(field * field), ("row", "col"))


def mix_modes(real_in, imag_in, spectral_weight, deep_count, freq_count):
    block = spectral_weight.reshape(2, deep_count, CHANNELS, CHANNELS, freq_count, KY)
    real_out = einsum_high("kcfg,kcofg->kofg", real_in, block[0]) - einsum_high(
        "kcfg,kcofg->kofg", imag_in, block[1]
    )
    imag_out = einsum_high("kcfg,kcofg->kofg", imag_in, block[0]) + einsum_high(
        "kcfg,kcofg->kofg", real_in, block[1]
    )
    return (real_out, imag_out)


def spectral_transpose(real_part, imag_part, spectral_weight, grid):
    rows, cols, n_row, n_col, row_id, col_id = grid
    full_rows = rows * n_row
    full_cols = cols * n_col
    cosine_rows, sine_rows = wave_table(
        signed_freqs(KX), jnp.arange(full_rows, dtype=jnp.int32), full_rows
    )
    cosine_cols, sine_cols = wave_table(
        signed_freqs(KY), jnp.arange(full_cols, dtype=jnp.int32), full_cols
    )
    real_part, imag_part = (
        lax.all_to_all(real_part, "row", split_axis=0, concat_axis=1, tiled=True),
        lax.all_to_all(imag_part, "row", split_axis=0, concat_axis=1, tiled=True),
    )
    first_real = einsum_high("qxy,xf->qfy", real_part, cosine_rows) + einsum_high(
        "qxy,xf->qfy", imag_part, sine_rows
    )
    first_imag = einsum_high("qxy,xf->qfy", imag_part, cosine_rows) - einsum_high(
        "qxy,xf->qfy", real_part, sine_rows
    )
    first_real, first_imag = (
        lax.all_to_all(first_real, "col", split_axis=1, concat_axis=2, tiled=True),
        lax.all_to_all(first_imag, "col", split_axis=1, concat_axis=2, tiled=True),
    )
    second_real = einsum_high("qfy,yg->qfg", first_real, cosine_cols) + einsum_high(
        "qfy,yg->qfg", first_imag, sine_cols
    )
    second_imag = einsum_high("qfy,yg->qfg", first_imag, cosine_cols) - einsum_high(
        "qfy,yg->qfg", first_real, sine_cols
    )
    deep_count = KZ // n_row
    freq_count = KX // n_col
    shape_in = (deep_count, CHANNELS, freq_count, KY)
    mixed_real, mixed_imag = mix_modes(
        second_real.reshape(shape_in),
        second_imag.reshape(shape_in),
        spectral_weight,
        deep_count,
        freq_count,
    )
    shape_out = (deep_count * CHANNELS, freq_count, KY)
    mixed_real = mixed_real.reshape(shape_out)
    mixed_imag = mixed_imag.reshape(shape_out)
    back_real = einsum_high("qfg,yg->qfy", mixed_real, cosine_cols) - einsum_high(
        "qfg,yg->qfy", mixed_imag, sine_cols
    )
    back_imag = einsum_high("qfg,yg->qfy", mixed_imag, cosine_cols) + einsum_high(
        "qfg,yg->qfy", mixed_real, sine_cols
    )
    back_real, back_imag = (
        lax.all_to_all(back_real, "col", split_axis=2, concat_axis=1, tiled=True),
        lax.all_to_all(back_imag, "col", split_axis=2, concat_axis=1, tiled=True),
    )
    out_real = einsum_high("qfy,xf->qxy", back_real, cosine_rows) - einsum_high(
        "qfy,xf->qxy", back_imag, sine_rows
    )
    out_imag = einsum_high("qfy,xf->qxy", back_imag, cosine_rows) + einsum_high(
        "qfy,xf->qxy", back_real, sine_rows
    )
    out_real, out_imag = (
        lax.all_to_all(out_real, "row", split_axis=1, concat_axis=0, tiled=True),
        lax.all_to_all(out_imag, "row", split_axis=1, concat_axis=0, tiled=True),
    )
    return (out_real, out_imag)


def precondition(residual, squares_total, log_perm, weights, grid, cells):
    lift_weight, spectral_weight, mix_weight, proj_weight = weights
    rows, cols, depth = residual.shape
    scale = jnp.sqrt(squares_total / cells + 1e-06)
    scaled = residual / scale
    lifted = jax.nn.gelu(
        lift_weight[:, 0, None, None, None] * scaled[None]
        + lift_weight[:, 1, None, None, None] * log_perm[None]
        + lift_weight[:, 2, None, None, None]
    )
    cosine_deep, sine_deep = wave_table(
        jnp.arange(KZ, dtype=jnp.int32), jnp.arange(depth, dtype=jnp.int32), depth
    )
    real_part = einsum_high("cxyz,zk->kcxy", lifted, cosine_deep).reshape(KZ * CHANNELS, rows, cols)
    imag_part = -einsum_high("cxyz,zk->kcxy", lifted, sine_deep).reshape(KZ * CHANNELS, rows, cols)
    out_real, out_imag = spectral_transpose(real_part, imag_part, spectral_weight, grid)
    out_real = out_real.reshape(KZ, CHANNELS, rows, cols)
    out_imag = out_imag.reshape(KZ, CHANNELS, rows, cols)
    spatial = (
        einsum_high("kcxy,zk->cxyz", out_real, cosine_deep)
        - einsum_high("kcxy,zk->cxyz", out_imag, sine_deep)
    ) / cells
    point = (
        einsum_high("oc,cxyz->oxyz", mix_weight[:, :CHANNELS], lifted)
        + mix_weight[:, CHANNELS, None, None, None]
    )
    hidden = jax.nn.gelu(spatial + point)
    return scale * (
        einsum_high("o,oxyz->xyz", proj_weight[:CHANNELS], hidden) + proj_weight[CHANNELS]
    )


def local(right_side, permeability, lift_weight, spectral_weight, mix_weight, proj_weight):
    rows, cols, depth = right_side.shape
    n_row = lax.axis_size("row")
    n_col = lax.axis_size("col")
    grid = (rows, cols, n_row, n_col, lax.axis_index("row"), lax.axis_index("col"))
    cells = float(rows * n_row * cols * n_col * depth)
    faces, log_perm = face_arrays(permeability)
    weights = (lift_weight, spectral_weight, mix_weight, proj_weight)

    def precond(residual, squares_total):
        return precondition(residual, squares_total, log_perm, weights, grid, cells)

    solution = jnp.zeros_like(right_side)
    residual = right_side
    kept = []
    update = precond(residual, global_squares(residual))
    kept.append(update)
    direction = update
    for step in range(ITERS):
        image = apply_operator(direction, faces)
        curvature, along = lax.psum(
            (jnp.sum(direction * image), jnp.sum(residual * direction)), ("row", "col")
        )
        alpha = along / curvature
        solution = solution + alpha * direction
        residual = residual - alpha * image
        if step + 1 < ITERS:
            update = precond(residual, global_squares(residual))
            kept.append(update)
            beta = lax.psum(jnp.sum(update * image), ("row", "col")) / curvature
            direction = update - beta * direction
    return (solution, residual, jnp.stack(kept))


def solution(mesh):
    placed = (
        P("row", "col", None),
        P("row", "col", None),
        P(),
        P(None, "row", None, None, "col"),
        P(),
        P(),
    )
    return jax.shard_map(
        local,
        mesh=mesh,
        in_specs=placed,
        out_specs=(P("row", "col", None), P("row", "col", None), P(None, "row", "col", None)),
        check_vma=False,
    )
```

profile of v0, /device:TPU:1, one launch (start us, length us, event | category | flops | bytes accessed | tf_op | source)
XLA Modules:
  0.0 819.3 jit_solution(3772809294178370734)
XLA Ops:
  4.4 68.7 %psum.49 = f32[]{:T(128)} all-reduce(f32[]{:T(128)} %multiply_reduce_fusion.14), channel_id=1, replica_groups=mesh['row'=16,'col'=8] {'row','col'}, use_global_device_ids=true, to_apply=%region_1.2 | all-reduce | flops 1 | bytes 8 | tf_op jit(solution)/shard_map/psum | solution.py:73
  75.0 10.7 %fusion.44 = f32[32,16,4,128]{3,0,2,1:T(8,128)S(1)} fusion(f32[16]{0:T(128)S(1)} %get-tuple-element.50, f32[4,128,256]{2,1,0:T(8,128)S(1)} %convert_log_fusion, f32[16]{0:T(128)S(1)} %get-tuple-element.51, f32[4,128,256]{2,1,0:T(8,128)S(1)} %broadcast_divide_fusion.1, f32[16]{0:T(128)S(1)} %get-tuple-element.49), kind=kOutput, calls=%fused_computation.54 | convolution fusion | flops 830586880 | bytes 2097344 | tf_op jit(solution)/shard_map/cxyz,zk->kcxy/dot_general | solution.py:30
  97.9 11.6 %fusion.46 = f32[32,16,4,128]{3,0,2,1:T(8,128)} fusion(f32[16]{0:T(128)S(1)} %get-tuple-element.50, f32[4,128,256]{2,1,0:T(8,128)S(1)} %convert_log_fusion, f32[16]{0:T(128)S(1)} %get-tuple-element.51, f32[4,128,256]{2,1,0:T(8,128)S(1)} %broadcast_divide_fusion.1, f32[16]{0:T(128)S(1)} %get-tuple-element.49), kind=kOutput, calls=%fused_computation.55 | convolution fusion | flops 830849024 | bytes 2097344 | tf_op jit(solution)/shard_map/cxyz,zk->kcxy/dot_general | solution.py:30
  122.7 7.2 all-to-all-start.1
  131.3 17.0 %fusion.36 = f32[4,128,256,16]{2,3,1,0:T(8,128)} fusion(f32[16,4,128,256]{3,2,1,0:T(8,128)} %fusion.8, f32[16,17]{1,0:T(8,128)S(1)} %copy-done.19), kind=kOutput, calls=%fused_computation.46 | convolution fusion | flops 402653184 | bytes 16778304 | tf_op jit(solution)/shard_map/oc,cxyz->oxyz/dot_general | solution.py:30
  214.6 7.0 all-to-all-start.6
  227.3 9.9 %all-to-all-done.6 = f32[32,64,128]{2,0,1:T(8,128)S(1)} async-done(((f32[32,64,128]{2,0,1:T(8,128)}), f32[32,64,128]{2,0,1:T(8,128)S(1)}, u32[]{:S(2)}, u32[]{:S(2)}) %all-to-all-start.6) | async-done | bytes 1048608 | tf_op jit(solution)/shard_map/all_to_all | solution.py:147
  251.3 9.2 %fusion.65 = f32[16,4,128,256]{3,2,1,0:T(8,128)} fusion(f32[32,16,4,128]{3,1,0,2:T(8,128)S(1)} %bitcast.349), kind=kOutput, calls=%fused_computation.95 | convolution fusion | flops 805421056 | bytes 9437184 | tf_op jit(solution)/shard_map/kcxy,zk->cxyz/dot_general | solution.py:30
  261.9 17.4 %fusion.15 = f32[16,4,128,256]{3,2,1,0:T(8,128)S(1)} fusion(f32[4,128,256,16]{2,3,1,0:T(8,128)} %fusion.36, f32[16,4,128,256]{3,2,1,0:T(8,128)} %fusion.65, f32[16]{0:T(128)S(1)} %copy-done.29, f32[32,16,4,128]{3,1,0,2:T(8,128)S(1)} %bitcast.374), kind=kOutput, calls=%fused_computation.21 | convolution fusion | flops 830586880 | bytes 26214464 | tf_op jit(solution)/shard_map/kcxy,zk->cxyz/dot_general | solution.py:30
  279.4 7.9 fusion.32
  305.2 70.0 %all-reduce.3 = (f32[]{:T(128)}, f32[]{:T(128)}) all-reduce(f32[]{:T(128)} %get-tuple-element.10, f32[]{:T(128)} %get-tuple-element.9), channel_id=1, replica_groups=mesh['row'=16,'col'=8] {'row','col'}, use_global_device_ids=true, to_apply=%region_3.4 | all-reduce | flops 2 | bytes 16 | tf_op jit(solution)/shard_map/psum | solution.py:205
  378.3 63.4 %psum.52 = f32[]{:T(128)} all-reduce(f32[]{:T(128)} %get-tuple-element.24), channel_id=1, replica_groups=mesh['row'=16,'col'=8] {'row','col'}, use_global_device_ids=true, to_apply=%region_7.8 | all-reduce | flops 1 | bytes 8 | tf_op jit(solution)/shard_map/psum | solution.py:73
  442.5 11.9 %fusion.40 = f32[32,16,4,128]{3,0,2,1:T(8,128)S(1)} fusion(f32[4,128,256]{2,1,0:T(8,128)S(1)} %broadcast_divide_fusion, f32[16]{0:T(128)S(1)} %copy-done.21, f32[4,128,256]{2,1,0:T(8,128)} %copy-done.6, f32[16]{0:T(128)S(1)} %copy-done.24, f32[16]{0:T(128)S(1)} %get-tuple-element.49), kind=kOutput, calls=%fused_computation.52 | convolution fusion | flops 830586880 | bytes 2097344 | tf_op jit(solution)/shard_map/cxyz,zk->kcxy/dot_general | solution.py:30
  460.8 11.7 %fusion.49 = f32[32,16,4,128]{3,0,2,1:T(8,128)S(1)} fusion(f32[4,128,256]{2,1,0:T(8,128)} %copy-done.14, f32[16]{0:T(128)S(1)} %copy-done.21, f32[4,128,256]{2,1,0:T(8,128)S(1)} %copy-done.7, f32[16]{0:T(128)S(1)} %copy-done.24, f32[16]{0:T(128)S(1)} %get-tuple-element.49), kind=kOutput, calls=%fused_computation.56 | convolution fusion | flops 830849024 | bytes 2097344 | tf_op jit(solution)/shard_map/cxyz,zk->kcxy/dot_general | solution.py:30
  483.8 12.9 %all-to-all-done.9 = f32[512,4,128]{2,1,0:T(4,128)} async-done(((f32[512,4,128]{2,1,0:T(4,128)}), f32[512,4,128]{2,1,0:T(4,128)}, u32[]{:S(2)}, u32[]{:S(2)}) %all-to-all-start.9) | async-done | bytes 1048608 | tf_op jit(solution)/shard_map/all_to_all | solution.py:99
  502.4 7.4 all-to-all-start.10
  582.2 6.8 fusion.22
  593.0 8.1 all-to-all-done.14
  605.6 17.0 %fusion.34 = f32[4,128,256,16]{2,3,1,0:T(8,128)} fusion(f32[16,4,128,256]{3,2,1,0:T(8,128)} %fusion.22, f32[16,17]{1,0:T(8,128)S(1)} %copy-done.19), kind=kOutput, calls=%fused_computation.43 | convolution fusion | flops 402653184 | bytes 16778304 | tf_op jit(solution)/shard_map/oc,cxyz->oxyz/dot_general | solution.py:30
  622.7 9.1 %fusion.62 = f32[16,4,128,256]{3,2,1,0:T(8,128)} fusion(f32[32,16,4,128]{3,1,0,2:T(8,128)S(1)} %bitcast.354), kind=kOutput, calls=%fused_computation.92 | convolution fusion | flops 805421056 | bytes 9437184 | tf_op jit(solution)/shard_map/kcxy,zk->cxyz/dot_general | solution.py:30
  633.2 17.8 %fusion.29 = f32[16,4,128,256]{3,2,1,0:T(8,128)S(1)} fusion(f32[4,128,256,16]{2,3,1,0:T(8,128)} %fusion.34, f32[16,4,128,256]{3,2,1,0:T(8,128)} %fusion.62, f32[16]{0:T(128)S(1)} %copy-done.30, f32[32,16,4,128]{3,1,0,2:T(8,128)S(1)} %bitcast.373), kind=kOutput, calls=%fused_computation.35 | convolution fusion | flops 830586880 | bytes 26214464 | tf_op jit(solution)/shard_map/kcxy,zk->cxyz/dot_general | solution.py:30
  651.1 7.7 fusion.30
  660.1 65.3 %psum.53 = f32[]{:T(128)} all-reduce(f32[]{:T(128)} %multiply_reduce_fusion.10), channel_id=1, replica_groups=mesh['row'=16,'col'=8] {'row','col'}, use_global_device_ids=true, to_apply=%region_9.10 | all-reduce | flops 1 | bytes 8 | tf_op jit(solution)/shard_map/psum | solution.py:214
  746.5 67.8 %all-reduce.2 = (f32[]{:T(128)}, f32[]{:T(128)}) all-reduce(f32[]{:T(128)} %get-tuple-element.4, f32[]{:T(128)} %get-tuple-element.3), channel_id=1, replica_groups=mesh['row'=16,'col'=8] {'row','col'}, use_global_device_ids=true, to_apply=%region_11.12 | all-reduce | flops 2 | bytes 16 | tf_op jit(solution)/shard_map/psum | solution.py:205
  (254 shorter events, 268.3 us)
Async XLA Ops:
  87.9 34.8 %all-to-all-start = ((f32[512,4,128]{2,1,0:T(4,128)}), f32[512,4,128]{2,1,0:T(4,128)S(1)}, u32[]{:S(2)}, u32[]{:S(2)}) async-start(f32[512,4,128]{2,1,0:T(4,128)} %copy.94), calls=%async_computation | async-start | bytes 2097152 | tf_op jit(solution)/shard_map/all_to_all | solution.py:98
  92.7 128.9 %collective-permute-start = (bf16[1,128,256]{2,1,0:T(8,128)(2,1)}, bf16[1,128,256]{2,1,0:T(8,128)(2,1)}, u32[]{:S(2)}, u32[]{:S(2)}) collective-permute-start(bf16[1,128,256]{2,1,0:T(8,128)(2,1)} %get-tuple-element.42), channel_id=1, source_target_pairs={{0,8},{8,16},{16,24},{24,32},{32,40},{40,48},{48,56},{56,64},{64,7... | collective-permute-start | bytes 196616 | tf_op jit(solution)/shard_map/ppermute | solution.py:21
  96.5 126.1 %collective-permute-start.1 = (bf16[1,128,256]{2,1,0:T(8,128)(2,1)}, bf16[1,128,256]{2,1,0:T(8,128)(2,1)}, u32[]{:S(2)}, u32[]{:S(2)}) collective-permute-start(bf16[1,128,256]{2,1,0:T(8,128)(2,1)} %get-tuple-element.41), channel_id=1, source_target_pairs={{8,0},{16,8},{24,16},{32,24},{40,32},{48,40},{56,48},{64,56},{72,6... | collective-permute-start | bytes 196616 | tf_op jit(solution)/shard_map/ppermute | solution.py:24
  122.7 26.3 %all-to-all-start.1 = ((f32[512,4,128]{2,1,0:T(4,128)}), f32[512,4,128]{2,1,0:T(4,128)}, u32[]{:S(2)}, u32[]{:S(2)}) async-start(f32[512,4,128]{2,1,0:T(4,128)} %copy.98), calls=%async_computation.1 | async-start | bytes 2097152 | tf_op jit(solution)/shard_map/all_to_all | solution.py:99
  153.9 11.9 %all-to-all-start.2 = ((f32[32,16,128]{2,0,1:T(8,128)}), f32[32,16,128]{2,0,1:T(8,128)S(1)}, u32[]{:S(2)}, u32[]{:S(2)}) async-start(f32[32,16,128]{2,0,1:T(8,128)} %copy.101), calls=%async_computation.2 | async-start | bytes 524288 | tf_op jit(solution)/shard_map/all_to_all | solution.py:108
  165.8 11.1 %all-to-all-start.3 = ((f32[32,16,128]{2,0,1:T(8,128)}), f32[32,16,128]{2,0,1:T(8,128)S(1)}, u32[]{:S(2)}, u32[]{:S(2)}) async-start(f32[32,16,128]{2,0,1:T(8,128)} %copy.103), calls=%async_computation.3 | async-start | bytes 524288 | tf_op jit(solution)/shard_map/all_to_all | solution.py:109
  187.0 10.9 %all-to-all-start.4 = ((f32[8,1,8192]{2,1,0:T(1,128)}), f32[8,1,8192]{2,1,0:T(1,128)S(1)}, u32[]{:S(2)}, u32[]{:S(2)}) async-start(f32[8,1,8192]{2,1,0:T(1,128)} %reshape.119), calls=%async_computation.4 | async-start | bytes 524288 | tf_op jit(solution)/shard_map/all_to_all | solution.py:137
  197.9 11.3 %all-to-all-start.5 = ((f32[8,1,8192]{2,1,0:T(1,128)}), f32[8,1,8192]{2,1,0:T(1,128)S(1)}, u32[]{:S(2)}, u32[]{:S(2)}) async-start(f32[8,1,8192]{2,1,0:T(1,128)} %reshape.121), calls=%async_computation.5 | async-start | bytes 524288 | tf_op jit(solution)/shard_map/all_to_all | solution.py:138
  214.6 22.7 %all-to-all-start.6 = ((f32[32,64,128]{2,0,1:T(8,128)}), f32[32,64,128]{2,0,1:T(8,128)S(1)}, u32[]{:S(2)}, u32[]{:S(2)}) async-start(f32[32,64,128]{2,0,1:T(8,128)} %copy.109), calls=%async_computation.6 | async-start | bytes 2097152 | tf_op jit(solution)/shard_map/all_to_all | solution.py:147
  237.3 23.3 %all-to-all-start.7 = ((f32[32,64,128]{2,0,1:T(8,128)}), f32[32,64,128]{2,0,1:T(8,128)}, u32[]{:S(2)}, u32[]{:S(2)}) async-start(f32[32,64,128]{2,0,1:T(8,128)} %copy.112), calls=%async_computation.7 | async-start | bytes 2097152 | tf_op jit(solution)/shard_map/all_to_all | solution.py:148
  241.7 8.1 collective-permute-start.3
  287.9 6.7 collective-permute-start.5
  289.2 6.3 collective-permute-start.4
  295.5 6.6 collective-permute-start.7
  456.7 20.1 %all-to-all-start.8 = ((f32[512,4,128]{2,1,0:T(4,128)}), f32[512,4,128]{2,1,0:T(4,128)S(1)}, u32[]{:S(2)}, u32[]{:S(2)}) async-start(f32[512,4,128]{2,1,0:T(4,128)} %copy.118), calls=%async_computation.8 | async-start | bytes 2097152 | tf_op jit(solution)/shard_map/all_to_all | solution.py:98
  476.8 19.8 %all-to-all-start.9 = ((f32[512,4,128]{2,1,0:T(4,128)}), f32[512,4,128]{2,1,0:T(4,128)}, u32[]{:S(2)}, u32[]{:S(2)}) async-start(f32[512,4,128]{2,1,0:T(4,128)} %copy.122), calls=%async_computation.9 | async-start | bytes 2097152 | tf_op jit(solution)/shard_map/all_to_all | solution.py:99
  502.4 14.0 %all-to-all-start.10 = ((f32[32,16,128]{2,0,1:T(8,128)}), f32[32,16,128]{2,0,1:T(8,128)}, u32[]{:S(2)}, u32[]{:S(2)}) async-start(f32[32,16,128]{2,0,1:T(8,128)} %copy.125), calls=%async_computation.10 | async-start | bytes 524288 | tf_op jit(solution)/shard_map/all_to_all | solution.py:108
  516.4 11.3 %all-to-all-start.11 = ((f32[32,16,128]{2,0,1:T(8,128)}), f32[32,16,128]{2,0,1:T(8,128)S(1)}, u32[]{:S(2)}, u32[]{:S(2)}) async-start(f32[32,16,128]{2,0,1:T(8,128)} %copy.127), calls=%async_computation.11 | async-start | bytes 524288 | tf_op jit(solution)/shard_map/all_to_all | solution.py:109
  542.4 11.6 %all-to-all-start.12 = ((f32[8,1,8192]{2,1,0:T(1,128)}), f32[8,1,8192]{2,1,0:T(1,128)}, u32[]{:S(2)}, u32[]{:S(2)}) async-start(f32[8,1,8192]{2,1,0:T(1,128)} %reshape.123), calls=%async_computation.12 | async-start | bytes 524288 | tf_op jit(solution)/shard_map/all_to_all | solution.py:137
  553.9 13.1 %all-to-all-start.13 = ((f32[8,1,8192]{2,1,0:T(1,128)}), f32[8,1,8192]{2,1,0:T(1,128)}, u32[]{:S(2)}, u32[]{:S(2)}) async-start(f32[8,1,8192]{2,1,0:T(1,128)} %reshape.125), calls=%async_computation.13 | async-start | bytes 524288 | tf_op jit(solution)/shard_map/all_to_all | solution.py:138
  578.5 22.5 %all-to-all-start.14 = ((f32[32,64,128]{2,0,1:T(8,128)}), f32[32,64,128]{2,0,1:T(8,128)S(1)}, u32[]{:S(2)}, u32[]{:S(2)}) async-start(f32[32,64,128]{2,0,1:T(8,128)} %copy.133), calls=%async_computation.14 | async-start | bytes 2097152 | tf_op jit(solution)/shard_map/all_to_all | solution.py:147
  601.0 30.8 %all-to-all-start.15 = ((f32[32,64,128]{2,0,1:T(8,128)}), f32[32,64,128]{2,0,1:T(8,128)}, u32[]{:S(2)}, u32[]{:S(2)}) async-start(f32[32,64,128]{2,0,1:T(8,128)} %copy.136), calls=%async_computation.15 | async-start | bytes 2097152 | tf_op jit(solution)/shard_map/all_to_all | solution.py:148
  728.4 6.3 collective-permute-start.9
  735.6 7.3 collective-permute-start.11
  (37 other events, 1518.3 us)
where the time goes:
time: 831 us; the launch traced here: 819 us
  blocking collectives  335 us (40%)
  matrix products  189 us (23%)
  starting transfers between devices  116 us (14%)
  waiting for transfers between devices  62.5 us (8%)
  local copies, waits for them, and re-layouts  61.9 us (7%)
  other arithmetic  47.3 us (6%)
    dot_general x44, matrix products, einsum_high(): return jnp.einsum(form, left, right, precision=HIGHEST)  189 us
    psum x2, blocking collectives, local(): lax.psum((jnp.sum(direction * image), jnp.sum(residual * direction)), ('r...  138 us
    psum x2, blocking collectives, global_squares(): return lax.psum(jnp.sum(field * field), ('row', 'col'))  132 us
    psum x1, blocking collectives, local(): beta = lax.psum(jnp.sum(update * image), ('row', 'col')) / curvature  65.3 us
    ppermute x6, starting transfers between devices, with_halo(): lax.ppermute(lax.slice_in_dim(block, block.shape[dim] - width, None, axis...  19.6 us
    all_to_all x2, waiting for transfers between devices, spectral_transpose(): lax.all_to_all(out_real, 'row', split_axis=1, concat_axis=0, tiled=True)  18 us
  transfers between devices with their start and end apart: 28, of which 16 were waited for; matrix products, arithmetic and copies ran while one was open for 20% of the time, Pallas kernels for 0%

commit v1 on v0

v1 whole, which is shorter than its diff:
```python
import jax
import jax.numpy as jnp
import ml_dtypes
import numpy as np
from jax import lax
from jax.experimental import pallas as pl
from jax.experimental.pallas import tpu as pltpu
from jax.sharding import PartitionSpec as P

F32 = jnp.float32
BF16 = jnp.bfloat16
MESH = pl.DeviceIdType.MESH
NR, NC = 16, 8
NX, NY, NZ = 64, 1024, 256
LX, LY = NX // NR, NY // NC
CH = 16
CELLS = float(NX * NY * NZ)
GELU_A = float(np.sqrt(2.0 / np.pi))


def pieces(table):
    high = table.astype(ml_dtypes.bfloat16)
    low = (table - high.astype(np.float64)).astype(ml_dtypes.bfloat16)
    return high, low


def waves(freqs, places, length):
    angle = 2.0 * np.pi * ((freqs[None, :] * places[:, None]) % length) / length
    return np.cos(angle), np.sin(angle)


def tables():
    cz, sz = waves(np.arange(32), np.arange(NZ), NZ)
    tz = np.zeros((LX, NZ, 2, 32, LX))
    ti = np.zeros((2, 32, LX, LX, NZ))
    for x in range(LX):
        tz[x, :, 0, :, x] = cz
        tz[x, :, 1, :, x] = sz
        ti[0, :, x, x, :] = cz.T
        ti[1, :, x, x, :] = -sz.T
    tz = pieces(tz.reshape(LX * NZ, 256))[0]
    ti_high, ti_low = pieces(ti.reshape(256, LX * NZ))
    ti = np.concatenate([ti_high, ti_high, ti_low], axis=0)

    yt = np.zeros((NC, 2, 32, 2, LY))
    yi = np.zeros((NC, 2, LY, 2, 32))
    for col in range(NC):
        cy, sy = waves(np.arange(-16, 16), np.arange(LY) + col * LY, NY)
        yt[col, 0, :, 0] = cy.T
        yt[col, 0, :, 1] = -sy.T
        yt[col, 1, :, 0] = -sy.T
        yt[col, 1, :, 1] = -cy.T
        yi[col, 0, :, 0] = cy
        yi[col, 0, :, 1] = -sy
        yi[col, 1, :, 0] = sy
        yi[col, 1, :, 1] = cy
    yt = np.concatenate(pieces(yt.reshape(NC, 64, 256)), axis=1)
    yi_high, yi_low = pieces(yi.reshape(NC, 256, 64))
    yi = np.concatenate([yi_high, yi_high, yi_low], axis=2)

    cx, sx = waves(np.arange(-8, 8), np.arange(NX), NX)
    cx = cx.reshape(NR, LX, NC, 2)
    sx = sx.reshape(NR, LX, NC, 2)
    xt = np.zeros((NC, 2, 2, 2, NR, 2, 2, LX))
    xi = np.zeros((NR, 2, 2, LX, NC, 2, 2, 2))
    for kz in range(2):
        forward_cos = cx.transpose(2, 3, 0, 1)
        forward_sin = sx.transpose(2, 3, 0, 1)
        xt[:, kz, :, 0, :, 0, kz, :] = forward_cos
        xt[:, kz, :, 0, :, 1, kz, :] = forward_sin
        xt[:, kz, :, 1, :, 1, kz, :] = forward_cos
        xt[:, kz, :, 1, :, 0, kz, :] = -forward_sin
        xi[:, 0, kz, :, :, kz, :, 0] = cx
        xi[:, 0, kz, :, :, kz, :, 1] = -sx
        xi[:, 1, kz, :, :, kz, :, 1] = cx
        xi[:, 1, kz, :, :, kz, :, 0] = sx
    xt = np.concatenate(pieces(xt.reshape(64, 256)), axis=0)
    xi_high, xi_low = pieces(xi.reshape(256, 64) * (0.5 / CELLS))
    xi = np.concatenate([xi_high, xi_high, xi_low], axis=1)

    fold = np.zeros((4, 4, 32, 4, 32))
    for r in range(4):
        for c in range(4):
            fold[r, c, :, r, :] = np.eye(32)
    fold = fold.reshape(512, 128)
    spread = np.ascontiguousarray(fold.T)
    gather = np.zeros((4, 4, 2, 4, 2, 16))
    for quad in range(4):
        for r in range(4):
            for ri in range(2):
                gather[quad, r, ri, r, ri, quad * 4 : quad * 4 + 4] = 1.0
    gather = gather.reshape(32, 128)
    left = np.kron(np.eye(16), np.ones((8, 1)))
    right = np.zeros((16, 16, 2, 8))
    for c in range(16):
        right[c, c] = 1.0
    right = right.reshape(16, 256)
    b16 = lambda a: a.astype(ml_dtypes.bfloat16)
    return tz, ti, yt, yi, xt, xi, b16(fold), b16(spread), b16(gather), b16(left), b16(right)


def split(value):
    high = value.astype(BF16)
    return high, (value - high.astype(F32)).astype(BF16)


def dot(left, right):
    return jnp.dot(left, right, preferred_element_type=F32)


def kernel(
    rs, perm, lw, mw, pw, mixv, weight,
    tz, ti, yt_all, yi_all, xt, xi, fold, spread, gather, left_map, right_map,
    sol, res, kept,
    lift, point, logp, padk, padp, faces, prev, image, fresh, maps, yt, yi,
    plx, phx, ply, phy,
    sf, vf, sx, vx, sm, vm, sh, vh, modes,
    asrc, acol, bsrc, arow, state,
    perm_s, perm_r, halo_s, halo_r, f_s, f_r, x_s, x_r, m_s, m_r, h_s, h_r, ac_s, ac_r, ar_s, ar_r, table_s,
):
    row = lax.axis_index("row")
    col = lax.axis_index("col")
    up_row, down_row = lax.rem(row + 1, NR), lax.rem(row + NR - 1, NR)
    up_col, down_col = lax.rem(col + 1, NC), lax.rem(col + NC - 1, NC)

    def send(src, dst, s, r, to_row, to_col):
        return pltpu.make_async_remote_copy(
            src_ref=src, dst_ref=dst, send_sem=s, recv_sem=r, device_id=(to_row, to_col), device_id_type=MESH
        )

    table_copies = [
        pltpu.make_async_copy(yt_all.at[col], yt, table_s.at[0]),
        pltpu.make_async_copy(yi_all.at[col], yi, table_s.at[1]),
    ]
    for copy in table_copies:
        copy.start()

    barrier = pltpu.get_barrier_semaphore()

    def greet_row(k, carry):
        pl.semaphore_signal(barrier, 1, device_id=(lax.rem(row + k, NR), col), device_id_type=MESH)
        return carry

    def greet_col(k, carry):
        pl.semaphore_signal(barrier, 1, device_id=(row, lax.rem(col + k, NC)), device_id_type=MESH)
        return carry

    lax.fori_loop(1, NR, greet_row, 0)
    lax.fori_loop(1, NC, greet_col, 0)
    pl.semaphore_wait(barrier, NR + NC - 2)

    perm_copies = [
        send(perm.at[LX - 1], plx, perm_s.at[0], perm_r.at[0], up_row, col),
        send(perm.at[0], phx, perm_s.at[1], perm_r.at[1], down_row, col),
        send(perm.at[:, pl.ds(LY - 16, 16), :], ply, perm_s.at[2], perm_r.at[2], row, up_col),
        send(perm.at[:, pl.ds(0, 16), :], phy, perm_s.at[3], perm_r.at[3], row, down_col),
    ]
    for copy in perm_copies:
        copy.start()

    def sums_begin(u, tile):
        asrc[u] = tile
        acol[u, col] = tile

        def step(k, carry):
            send(asrc.at[u], acol.at[u, col], ac_s.at[u], ac_r.at[u], row, lax.rem(col + k, NC)).start()
            return carry

        lax.fori_loop(1, NC, step, 0)

    def sums_end(u):
        whole = send(acol.at[u, pl.ds(0, NC - 1)], acol.at[u, pl.ds(0, NC - 1)], ac_s.at[u], ac_r.at[u], row, col)
        whole.wait_recv()
        whole.wait_send()
        tile = jnp.sum(acol[u], axis=0)
        bsrc[u] = tile
        arow[u, row] = tile

        def step(k, carry):
            send(bsrc.at[u], arow.at[u, row], ar_s.at[u], ar_r.at[u], lax.rem(row + k, NR), col).start()
            return carry

        lax.fori_loop(1, NR, step, 0)
        whole = send(arow.at[u, pl.ds(0, NR - 1)], arow.at[u, pl.ds(0, NR - 1)], ar_s.at[u], ar_r.at[u], row, col)
        whole.wait_recv()
        whole.wait_send()
        return jnp.sum(jnp.sum(arow[u], axis=0), axis=1, keepdims=True)

    def tile_of(parts):
        rows = []
        for part in parts:
            line = jnp.sum(part, axis=0, keepdims=True)
            rows.append(line[:, :128] + line[:, 128:])
        index = lax.broadcasted_iota(jnp.int32, (8, 128), 0)
        tile = jnp.zeros((8, 128), F32)
        for i, line in enumerate(rows):
            tile = jnp.where(index == i, jnp.broadcast_to(line, (8, 128)), tile)
        return tile

    def first_pass(b, total):
        x, y = lax.div(b, 4), pl.multiple_of(lax.rem(b, 4) * 32, 32)
        value = rs[x, pl.ds(y, 32), :]
        res[x, pl.ds(y, 32), :] = value
        squares = value * value
        return total + (squares[0:8] + squares[8:16]) + (squares[16:24] + squares[24:32])

    total = lax.fori_loop(0, 16, first_pass, jnp.zeros((8, NZ), F32))
    sums_begin(0, tile_of([total]))

    def second_pass(b, carry):
        x, y = lax.div(b, 4), pl.multiple_of(lax.rem(b, 4) * 32, 32)
        value = perm[x, pl.ds(y, 32), :].astype(F32)
        padp[x + 1, pl.ds(pl.multiple_of(y + 8, 8), 32), :] = value
        logp[x, pl.ds(y, 32), :] = jnp.log(value)
        zero = jnp.zeros((32, NZ), F32)
        sol[x, pl.ds(y, 32), :] = zero
        prev[x, pl.ds(y, 32), :] = zero
        image[x, pl.ds(y, 32), :] = zero
        return carry

    lax.fori_loop(0, 16, second_pass, 0)
    mix_high, mix_low = split(mixv[:, 0:CH] * 0.5)
    rows_iota = lax.broadcasted_iota(jnp.int32, (128, 256), 0)
    lane_iota = lax.broadcasted_iota(jnp.int32, (128, 256), 1)
    same = lax.rem(rows_iota, 8) == lax.rem(lane_iota, 8)
    for n, piece in enumerate((mix_high, mix_low)):
        wide = dot(left_map[...], dot(piece, right_map[...]).astype(BF16))
        maps[n * 128 : (n + 1) * 128, :] = jnp.where(same, wide, 0.0).astype(BF16)

    for copy in perm_copies:
        copy.wait()
    padp[0, pl.ds(8, LY), :] = plx[...].astype(F32)
    padp[LX + 1, pl.ds(8, LY), :] = phx[...].astype(F32)
    for x in range(LX):
        padp[x + 1, pl.ds(0, 8), :] = ply[x].astype(F32)[8:16]
        padp[x + 1, pl.ds(LY + 8, 8), :] = phy[x].astype(F32)[0:8]

    @pl.when(row == 0)
    def _():
        padp[0, pl.ds(8, LY), :] = padp[1, pl.ds(8, LY), :]

    @pl.when(row == NR - 1)
    def _():
        padp[LX + 1, pl.ds(8, LY), :] = padp[LX, pl.ds(8, LY), :]

    @pl.when(col == 0)
    def _():
        for x in range(LX):
            padp[x + 1, pl.ds(0, 8), :] = jnp.broadcast_to(padp[x + 1, pl.ds(8, 8), :][0:1], (8, NZ))

    @pl.when(col == NC - 1)
    def _():
        for x in range(LX):
            padp[x + 1, pl.ds(LY + 8, 8), :] = jnp.broadcast_to(padp[x + 1, pl.ds(LY, 8), :][7:8], (8, NZ))

    lanes = lax.broadcasted_iota(jnp.int32, (32, NZ), 1)

    def around(ref, x, y, edge):
        own = ref[x + 1, pl.ds(y, 48), :]
        here = own[8:40]
        before = pltpu.roll(here, 1, 1)
        after = pltpu.roll(here, NZ - 1, 1)
        if edge:
            before = jnp.where(lanes == 0, here, before)
            after = jnp.where(lanes == NZ - 1, here, after)
        else:
            before = jnp.where(lanes == 0, 0.0, before)
            after = jnp.where(lanes == NZ - 1, 0.0, after)
        return here, (
            ref[x, pl.ds(pl.multiple_of(y + 8, 8), 32), :], ref[x + 2, pl.ds(pl.multiple_of(y + 8, 8), 32), :], own[7:39], own[9:41], before, after
        )

    def face_pass(b, carry):
        x, y = lax.div(b, 4), pl.multiple_of(lax.rem(b, 4) * 32, 32)
        here, others = around(padp, x, y, True)
        for n, other in enumerate(others):
            faces[n, x, pl.ds(y, 32), :] = 2.0 * here * other / (here + other)
        return carry

    lax.fori_loop(0, 16, face_pass, 0)

    for copy in table_copies:
        copy.wait()
    state[0] = jnp.broadcast_to(sums_end(0)[0:1], (8, 128))
    state[1] = jnp.ones((8, 128), F32)

    mask_rows = lax.broadcasted_iota(jnp.int32, (16, 128), 0)
    mask_lanes = lax.broadcasted_iota(jnp.int32, (16, 128), 1)
    quad_mask = lax.rem(mask_rows, 4) == mask_lanes // 32
    low_half = lax.broadcasted_iota(jnp.int32, (8, 128), 0) < 4

    def iteration(i, carry):
        mean = state[0][0:1, 0:1] * (1.0 / CELLS) + 1e-6
        scale = jnp.sqrt(mean)
        inverse = 1.0 / scale

        def forward(cq, carry):
            def lift_pass(b, carry):
                x, y = lax.div(b, 16), pl.multiple_of(lax.rem(b, 16) * 8, 8)
                scaled = res[x, pl.ds(y, 8), :] * inverse
                logs = logp[x, pl.ds(y, 8), :]
                for c4 in range(4):
                    c = cq * 4 + c4
                    half = (lw[c, 0] * 0.5) * scaled + (lw[c, 1] * 0.5) * logs + lw[c, 2] * 0.5
                    inner = half * (2.0 * GELU_A + (8.0 * 0.044715 * GELU_A) * (half * half))
                    value = half + half * jnp.tanh(inner)
                    rest = value - value.astype(BF16).astype(F32)
                    lift[b, c] = jnp.concatenate([value, rest], axis=0).astype(BF16)
                return carry

            lax.fori_loop(0, 64, lift_pass, 0)
            tops, bottoms = [], []
            for c4 in range(4):
                c = cq * 4 + c4
                block = jnp.concatenate(
                    [lift[x * 16 : x * 16 + 16, c].reshape(256, NZ) for x in range(LX)], axis=1
                )
                deep = dot(block, tz[...]).reshape(16, 2, 8, 256)
                deep = (deep[:, 0] + deep[:, 1]).reshape(128, 256)
                tops.append(deep[:, :128])
                bottoms.append(deep[:, 128:])
            high, low = split(
                jnp.concatenate([jnp.concatenate(tops, axis=1), jnp.concatenate(bottoms, axis=1)], axis=0)
            )
            both = dot(yt[...], high)
            flat = both[:64] + both[64:] + dot(yt[0:64, :], low)
            for ri in range(2):
                square = jnp.concatenate(
                    [flat[ri * 32 : ri * 32 + 32, c4 * 128 : c4 * 128 + 128] for c4 in range(4)], axis=0
                )
                sf[cq, :, pl.ds(ri * 8, 8), :] = square.T.reshape(NR, 8, 128)
            vf[cq, row] = sf[cq, row]

            def step(k, carry):
                to = lax.rem(row + k, NR)
                send(sf.at[cq, to], vf.at[cq, row], f_s.at[cq], f_r.at[cq], to, col).start()
                return carry

            lax.fori_loop(1, NR, step, 0)
            return carry

        lax.fori_loop(0, 4, forward, 0)

        def point_pass(b, carry):
            x, y = lax.div(b, 16), lax.rem(b, 16)
            both = dot(maps[...], lift[b].reshape(256, NZ))
            point[x, y] = (both[:128] + both[128:]).reshape(CH, 8, NZ)
            return carry

        lax.fori_loop(0, 64, point_pass, 0)

        blocks = []
        for cq in range(4):
            whole = send(
                sf.at[cq, pl.ds(0, NR - 1)], vf.at[cq, pl.ds(0, NR - 1)], f_s.at[cq], f_r.at[cq], row, col
            )
            whole.wait_recv()
            whole.wait_send()
            blocks.append(vf[cq].reshape(256, 128))
        high, low = split(jnp.concatenate(blocks, axis=1))
        both = dot(xt[...], high)
        partial = both[:64] + both[64:] + dot(xt[0:64, :], low)
        sx[...] = partial.reshape(NC, 8, 512)
        vx[col] = sx[col]

        def scatter(k, carry):
            to = lax.rem(col + k, NC)
            send(sx.at[to], vx.at[col], x_s, x_r, row, to).start()
            return carry

        lax.fori_loop(1, NC, scatter, 0)
        whole = send(sx.at[pl.ds(0, NC - 1)], vx.at[pl.ds(0, NC - 1)], x_s, x_r, row, col)
        whole.wait_recv()
        whole.wait_send()
        spectrum = jnp.sum(vx[...], axis=0)

        stacks = []
        for ri in range(2):
            tiles = []
            for r in range(4):
                line = r * 2 + ri
                wide = [
                    jnp.broadcast_to(spectrum[line : line + 1, q * 128 : q * 128 + 128], (8, 128)) for q in range(4)
                ]
                tall = jnp.concatenate(
                    [jnp.where(low_half, wide[0], wide[1]), jnp.where(low_half, wide[2], wide[3])], axis=0
                )
                tiles.append(jnp.where(quad_mask, tall, 0.0))
            stacks.append(jnp.concatenate(tiles, axis=1))
        high, low = split(jnp.concatenate(stacks, axis=0))
        both = dot(jnp.concatenate([high, low], axis=0), fold[...])
        ordered = both[:32] + both[32:]

        reals, imags = [], []
        for kz in range(2):
            real = jnp.zeros((CH, 64), F32)
            imag = jnp.zeros((CH, 64), F32)
            for c in range(CH):
                value_real = ordered[c : c + 1, kz * 64 : kz * 64 + 64]
                value_imag = ordered[CH + c : CH + c + 1, kz * 64 : kz * 64 + 64]
                weight_real = weight[0, kz, c]
                weight_imag = weight[1, kz, c]
                real = real + (weight_real * value_real - weight_imag * value_imag)
                imag = imag + (weight_real * value_imag + weight_imag * value_real)
            reals.append(real)
            imags.append(imag)
        mixed = jnp.concatenate([jnp.concatenate(reals, axis=1), jnp.concatenate(imags, axis=1)], axis=0)

        high, low = split(mixed)
        both = dot(jnp.concatenate([high, low], axis=0), spread[...])
        wide = both[:32] + both[32:]
        mask = jnp.concatenate([quad_mask, quad_mask], axis=0)
        tall = jnp.concatenate(
            [jnp.where(mask, wide[:, r * 128 : r * 128 + 128], 0.0) for r in range(4)], axis=0
        )
        high, low = split(tall)
        both = dot(gather[...], jnp.concatenate([high, low], axis=1))
        sm[...] = (both[:, :128] + both[:, 128:]).reshape(4, 8, 128)
        vm[col] = sm[...]

        def spread_out(k, carry):
            send(sm, vm.at[col], m_s, m_r, row, lax.rem(col + k, NC)).start()
            return carry

        lax.fori_loop(1, NC, spread_out, 0)
        whole = send(vm.at[pl.ds(0, NC - 1)], vm.at[pl.ds(0, NC - 1)], m_s, m_r, row, col)
        whole.wait_recv()
        whole.wait_send()

        high, low = split(jnp.concatenate([vm[:, oq].reshape(64, 128) for oq in range(4)], axis=1))
        back = dot(xi[...], jnp.concatenate([high, low, high], axis=0))
        for oq in range(4):
            sh[oq] = back[:, oq * 128 : oq * 128 + 128].reshape(NR, 16, 128)
            vh[oq, row] = sh[oq, row]

            def step(k, carry, oq=oq):
                to = lax.rem(row + k, NR)
                send(sh.at[oq, to], vh.at[oq, row], h_s.at[oq], h_r.at[oq], to, col).start()
                return carry

            lax.fori_loop(1, NR, step, 0)

        def clear(b, carry):
            x, y = lax.div(b, 4), pl.multiple_of(lax.rem(b, 4) * 32, 32)
            padk[x + 1, pl.ds(pl.multiple_of(y + 8, 8), 32), :] = jnp.full((32, NZ), pw[CH], F32)
            return carry

        lax.fori_loop(0, 16, clear, 0)

        def backward(oq, carry):
            whole = send(
                sh.at[oq, pl.ds(0, NR - 1)], vh.at[oq, pl.ds(0, NR - 1)], h_s.at[oq], h_r.at[oq], row, col
            )
            whole.wait_recv()
            whole.wait_send()
            turned = [vh[oq, :, pl.ds(ri * 8, 8), :].reshape(128, 128).T for ri in range(2)]
            block = jnp.concatenate(
                [
                    jnp.concatenate([turned[ri][o4 * 32 : o4 * 32 + 32] for ri in range(2)], axis=0)
                    for o4 in range(4)
                ],
                axis=1,
            )
            high, low = split(block)
            back = dot(yi[...], jnp.concatenate([high, low, high], axis=0))
            for o4 in range(4):
                part = back[:, o4 * 128 : o4 * 128 + 128]
                high, low = split(jnp.concatenate([part[:128], part[128:]], axis=1))
                modes[o4] = jnp.concatenate([high, low, high], axis=1)

            for x in range(LX):
                for o4 in range(4):
                    o = oq * 4 + o4
                    bias = mw[o, CH] * 0.5
                    weight_out = pw[o]
                    wave = dot(modes[o4], ti[:, x * NZ : x * NZ + NZ])
                    half = wave + point[x, :, o].reshape(128, NZ) + bias
                    inner = half * (2.0 * GELU_A + (8.0 * 0.044715 * GELU_A) * (half * half))
                    hidden = weight_out * (half + half * jnp.tanh(inner))
                    padk[x + 1, pl.ds(8, LY), :] += hidden
            return carry

        lax.fori_loop(0, 4, backward, 0)

        def finish(b, carry):
            x, y = lax.div(b, 4), pl.multiple_of(lax.rem(b, 4) * 32, 32)
            value = scale * padk[x + 1, pl.ds(pl.multiple_of(y + 8, 8), 32), :]
            padk[x + 1, pl.ds(pl.multiple_of(y + 8, 8), 32), :] = value
            kept[i, x, pl.ds(y, 32), :] = value
            return carry

        lax.fori_loop(0, 16, finish, 0)

        copies = [
            send(padk.at[LX, pl.ds(8, LY)], padk.at[0, pl.ds(8, LY)], halo_s.at[0], halo_r.at[0], up_row, col),
            send(padk.at[1, pl.ds(8, LY)], padk.at[LX + 1, pl.ds(8, LY)], halo_s.at[1], halo_r.at[1], down_row, col),
            send(
                padk.at[pl.ds(1, LX), pl.ds(LY, 8)], padk.at[pl.ds(1, LX), pl.ds(0, 8)],
                halo_s.at[2], halo_r.at[2], row, up_col,
            ),
            send(
                padk.at[pl.ds(1, LX), pl.ds(8, 8)], padk.at[pl.ds(1, LX), pl.ds(LY + 8, 8)],
                halo_s.at[3], halo_r.at[3], row, down_col,
            ),
        ]
        for copy in copies:
            copy.start()
        for copy in copies:
            copy.wait()

        @pl.when(row == 0)
        def _():
            padk[0, pl.ds(8, LY), :] = jnp.zeros((LY, NZ), F32)

        @pl.when(row == NR - 1)
        def _():
            padk[LX + 1, pl.ds(8, LY), :] = jnp.zeros((LY, NZ), F32)

        @pl.when(col == 0)
        def _():
            padk[pl.ds(1, LX), pl.ds(0, 8), :] = jnp.zeros((LX, 8, NZ), F32)

        @pl.when(col == NC - 1)
        def _():
            padk[pl.ds(1, LX), pl.ds(LY + 8, 8), :] = jnp.zeros((LX, 8, NZ), F32)

        def fold8(value):
            return (value[0:8] + value[8:16]) + (value[16:24] + value[24:32])

        def operator_pass(b, totals):
            x, y = lax.div(b, 4), pl.multiple_of(lax.rem(b, 4) * 32, 32)
            here, others = around(padk, x, y, False)
            applied = jnp.zeros((32, NZ), F32)
            for n, other in enumerate(others):
                applied = applied + faces[n, x, pl.ds(y, 32), :] * (here - other)
            fresh[x, pl.ds(y, 32), :] = applied
            old_image = image[x, pl.ds(y, 32), :]
            residual = res[x, pl.ds(y, 32), :]
            old = prev[x, pl.ds(y, 32), :]
            terms = (
                here * applied, here * old_image, residual * here, residual * old, residual * applied,
                applied * applied,
            )
            return tuple(total + fold8(term) for total, term in zip(totals, terms))

        totals = lax.fori_loop(0, 16, operator_pass, tuple(jnp.zeros((8, NZ), F32) for _ in range(6)))
        sums_begin(1 + i, tile_of(totals))
        sums = sums_end(1 + i)
        k_ak, k_img, r_k, r_d, r_ak, ak_ak = [sums[n : n + 1] for n in range(6)]
        old_curve = state[1][0:1, 0:1]
        beta = k_img / old_curve
        curve = k_ak - 2.0 * beta * k_img + beta * beta * old_curve
        alpha = (r_k - beta * r_d) / curve

        def update(b, carry):
            x, y = lax.div(b, 4), pl.multiple_of(lax.rem(b, 4) * 32, 32)
            at = (x, pl.ds(y, 32), slice(None))
            direction = padk[x + 1, pl.ds(pl.multiple_of(y + 8, 8), 32), :] - beta * prev[at]
            applied = fresh[at] - beta * image[at]
            prev[at] = direction
            image[at] = applied
            sol[at] = sol[at] + alpha * direction
            res[at] = res[at] - alpha * applied
            return carry

        lax.fori_loop(0, 16, update, 0)
        squares = state[0][0:1, 0:1] - 2.0 * alpha * r_ak + alpha * alpha * ak_ak
        state[0] = jnp.broadcast_to(jnp.maximum(squares, 0.0), (8, 128))
        state[1] = jnp.broadcast_to(curve, (8, 128))
        return carry

    lax.fori_loop(0, 2, iteration, 0)


def local(right_side, permeability, lift_weight, spectral_weight, mix_weight, proj_weight):
    vmem = pl.BlockSpec(memory_space=pltpu.VMEM)
    smem = pl.BlockSpec(memory_space=pltpu.SMEM)
    hbm = pl.BlockSpec(memory_space=pl.ANY)
    field = (LX, LY, NZ)
    dma = pltpu.SemaphoreType.DMA
    scratch = [
        pltpu.VMEM((64, CH, 16, NZ), BF16),
        pltpu.VMEM((LX, 16, CH, 8, NZ), F32),
        pltpu.VMEM(field, F32),
        pltpu.VMEM((LX + 2, LY + 16, NZ), F32),
        pltpu.VMEM((LX + 2, LY + 16, NZ), F32),
        pltpu.VMEM((6,) + field, F32),
        pltpu.VMEM(field, F32),
        pltpu.VMEM(field, F32),
        pltpu.VMEM(field, F32),
        pltpu.VMEM((256, 256), BF16),
        pltpu.VMEM((128, 256), BF16),
        pltpu.VMEM((256, 192), BF16),
        pltpu.VMEM((LY, NZ), BF16),
        pltpu.VMEM((LY, NZ), BF16),
        pltpu.VMEM((LX, 16, NZ), BF16),
        pltpu.VMEM((LX, 16, NZ), BF16),
        pltpu.VMEM((4, NR, 16, 128), F32),
        pltpu.VMEM((4, NR, 16, 128), F32),
        pltpu.VMEM((NC, 8, 512), F32),
        pltpu.VMEM((NC, 8, 512), F32),
        pltpu.VMEM((4, 8, 128), F32),
        pltpu.VMEM((NC, 4, 8, 128), F32),
        pltpu.VMEM((4, NR, 16, 128), F32),
        pltpu.VMEM((4, NR, 16, 128), F32),
        pltpu.VMEM((4, LY, 768), BF16),
        pltpu.VMEM((3, 8, 128), F32),
        pltpu.VMEM((3, NC, 8, 128), F32),
        pltpu.VMEM((3, 8, 128), F32),
        pltpu.VMEM((3, NR, 8, 128), F32),
        pltpu.VMEM((2, 8, 128), F32),
        dma((4,)), dma((4,)), dma((4,)), dma((4,)), dma((4,)), dma((4,)),
        dma, dma, dma, dma, dma((4,)), dma((4,)),
        dma((3,)), dma((3,)), dma((3,)), dma((3,)), dma((2,)),
    ]
    constants = [jnp.asarray(t) for t in tables()]
    return pl.pallas_call(
        kernel,
        out_shape=[
            jax.ShapeDtypeStruct(field, F32),
            jax.ShapeDtypeStruct(field, F32),
            jax.ShapeDtypeStruct((2,) + field, F32),
        ],
        in_specs=[vmem, vmem, smem, smem, smem, vmem, vmem, vmem, vmem, hbm, hbm] + [vmem] * 7,
        out_specs=[vmem, vmem, vmem],
        scratch_shapes=scratch,
        compiler_params=pltpu.CompilerParams(
            collective_id=0, has_side_effects=True, vmem_limit_bytes=56 * 1024 * 1024
        ),
    )(
        right_side, permeability, lift_weight, mix_weight, proj_weight, mix_weight,
        spectral_weight, *constants,
    )


def solution(mesh):
    placed = (
        P("row", "col", None), P("row", "col", None), P(), P(None, "row", None, None, "col"), P(), P(),
    )
    return jax.shard_map(
        local,
        mesh=mesh,
        in_specs=placed,
        out_specs=(P("row", "col", None), P("row", "col", None), P(None, "row", "col", None)),
        check_vma=False,
    )
```

time: 831 us -> 170 us (0.20); the launches traced: 819 us -> 170 us
  blocking collectives: 335 us -> 0 us
  matrix products: 189 us -> 0 us
  Pallas kernels: 0 us -> 163 us
  starting transfers between devices: 116 us -> 0 us
  waiting for transfers between devices: 62.5 us -> 0 us
  local copies, waits for them, and re-layouts: 61.9 us -> 6.15 us
  other arithmetic: 47.3 us -> 0 us
    psum x5 -> x0, blocking collectives: 335 us -> none  [the longest x2 138 us: local(): lax.psum((jnp.sum(direction * image), jnp.sum(residual * direction)), ('r...]
    dot_general x44 -> x0, matrix products: 189 us -> none  [einsum_high(): return jnp.einsum(form, left, right, precision=HIGHEST)]
    pallas_call x0 -> x1, Pallas kernels: none -> 163 us  [local(): pl.pallas_call(kernel, out_shape=[jax.ShapeDtypeStruct(field, F32), jax.S...]
    all_to_all x16 -> x0, starting transfers between devices: 81.1 us -> none  [the longest x2 12.7 us: spectral_transpose(): lax.all_to_all(first_real, 'col', split_axis=1, concat_axis=2, tiled=True)]
    all_to_all x16 -> x0, waiting for transfers between devices: 58.5 us -> none  [the longest x2 18 us: spectral_transpose(): lax.all_to_all(out_real, 'row', split_axis=1, concat_axis=0, tiled=True)]
    ppermute x12 -> x0, starting transfers between devices: 35.4 us -> none  [the longest x6 19.6 us: with_halo(): lax.ppermute(lax.slice_in_dim(block, block.shape[dim] - width, None, axis...]
    all_to_all x25 -> x0, local copies, waits for them, and re-layouts: 15.9 us -> none  [the longest x4 3.94 us: spectral_transpose(): lax.all_to_all(imag_part, 'row', split_axis=0, concat_axis=1, tiled=True)]
    mul x3 -> x0, other arithmetic: 13.1 us -> none  [the longest x2 12.4 us: precondition(): jax.nn.gelu(lift_weight[:, 0, None, None, None] * scaled[None] + lift_wei...]
  transfers between devices with their start and end apart: 28 -> 0, of which waited for: 16 -> 0; matrix products, arithmetic and copies ran while one was open for 20% -> 0% of each run, Pallas kernels for 0% -> 0%
where the time goes in v1:
time: 170 us
  Pallas kernels  163 us (96%)
  local copies, waits for them, and re-layouts  6.15 us (4%)
    pallas_call x1, Pallas kernels, local(): pl.pallas_call(kernel, out_shape=[jax.ShapeDtypeStruct(field, F32), jax.S...  163 us
    unnamed x6, local copies, waits for them, and re-layouts  6.15 us

profile of v1, /device:TPU:1, one launch (start us, length us, event | category | flops | bytes accessed | tf_op | source)
XLA Modules:
  0.0 170.0 jit_solution(11390151441986818698)
XLA Ops:
  0.6 1.4 copy.20.lw
  2.0 163.2 %shard_map.184 = (f32[4,128,256]{2,1,0:T(8,128)}, f32[4,128,256]{2,1,0:T(8,128)}, f32[2,4,128,256]{3,2,1,0:T(8,128)}) custom-call(f32[4,128,256]{2,1,0:T(8,128)} %rs.1, bf16[4,128,256]{2,1,0:T(8,128)(2,1)} %perm.1, f32[16,3]{1,0:T(8,128)} %copy.20.lw, f32[16,17]{1,0:T(8,128)} %mixv.1, f32[17]{0:T(128)} %pw.1, f32[16,17]{1,0:T(8,128)} %mixv.1, ...), custom_call_target="tpu_custom_call" | custom-call | tf_op jit(solution)/shard_map/pallas_call | solution.py:617
  165.2 0.0 copy-start
  165.2 2.0 %copy.24 = f32[4,128,256]{2,1,0:T(8,128)} copy(f32[4,128,256]{2,1,0:T(8,128)} %get-tuple-element.6) | data formatting | bytes 1048576
  167.1 1.9 %copy.25 = f32[4,128,256]{2,1,0:T(8,128)} copy(f32[4,128,256]{2,1,0:T(8,128)} %get-tuple-element.7) | data formatting | bytes 1048576
  169.0 0.0 copy-done
  169.0 1.0 copy.26
Async XLA Ops:
  165.2 3.8 %copy-start = (f32[2,4,128,256]{3,2,1,0:T(8,128)S(1)}, f32[2,4,128,256]{3,2,1,0:T(8,128)}, u32[]{:S(2)}) copy-start(f32[2,4,128,256]{3,2,1,0:T(8,128)} %get-tuple-element.8) | copy-start | bytes 3145732

commit v2 on v1

--- a/solution.py
+++ b/solution.py
@@ -41,6 +41,7 @@
     tz = pieces(tz.reshape(LX * NZ, 256))[0]
     ti_high, ti_low = pieces(ti.reshape(256, LX * NZ))
     ti = np.concatenate([ti_high, ti_high, ti_low], axis=0)
+    ti = np.ascontiguousarray(ti.reshape(768, LX, NZ).transpose(1, 0, 2))
 
     yt = np.zeros((NC, 2, 32, 2, LY))
     yi = np.zeros((NC, 2, LY, 2, 32))
@@ -109,14 +110,15 @@
 
 
 def kernel(
-    rs, perm, lw, mw, pw, mixv, weight,
-    tz, ti, yt_all, yi_all, xt, xi, fold, spread, gather, left_map, right_map,
-    sol, res, kept,
+    rs, perm_in, lw, mw, pw, mix_in, weight_in,
+    tz_in, ti_in, yt_all, yi_all, xt_in, xi_in, fold_in, spread_in, gather_in, left_in, right_in,
+    kept_out, image_out, steps_out,
+    res, perm, mixv, weight, tz, ti, xt, xi, fold, spread, gather, left_map, right_map,
     lift, point, logp, padk, padp, faces, prev, image, fresh, maps, yt, yi,
     plx, phx, ply, phy,
     sf, vf, sx, vx, sm, vm, sh, vh, modes,
     asrc, acol, bsrc, arow, state,
-    perm_s, perm_r, halo_s, halo_r, f_s, f_r, x_s, x_r, m_s, m_r, h_s, h_r, ac_s, ac_r, ar_s, ar_r, table_s,
+    perm_s, perm_r, halo_s, halo_r, f_s, f_r, x_s, x_r, m_s, m_r, h_s, h_r, ac_s, ac_r, ar_s, ar_r, table_s, kept_s, image_s,
 ):
     row = lax.axis_index("row")
     col = lax.axis_index("col")
@@ -128,11 +130,13 @@
             src_ref=src, dst_ref=dst, send_sem=s, recv_sem=r, device_id=(to_row, to_col), device_id_type=MESH
         )
 
-    table_copies = [
-        pltpu.make_async_copy(yt_all.at[col], yt, table_s.at[0]),
-        pltpu.make_async_copy(yi_all.at[col], yi, table_s.at[1]),
+    loads = [
+        (rs, res), (perm_in, perm), (mix_in, mixv), (left_in, left_map), (right_in, right_map), (tz_in, tz),
+        (yt_all.at[col], yt), (xt_in, xt), (weight_in, weight), (fold_in, fold), (spread_in, spread),
+        (gather_in, gather), (xi_in, xi), (yi_all.at[col], yi), (ti_in, ti),
     ]
-    for copy in table_copies:
+    loads = [pltpu.make_async_copy(src, dst, table_s.at[n]) for n, (src, dst) in enumerate(loads)]
+    for copy in loads:
         copy.start()
 
     barrier = pltpu.get_barrier_semaphore()
@@ -145,15 +149,15 @@
         pl.semaphore_signal(barrier, 1, device_id=(row, lax.rem(col + k, NC)), device_id_type=MESH)
         return carry
 
-    lax.fori_loop(1, NR, greet_row, 0)
-    lax.fori_loop(1, NC, greet_col, 0)
+    lax.fori_loop(1, NR, greet_row, 0, unroll=True)
+    lax.fori_loop(1, NC, greet_col, 0, unroll=True)
     pl.semaphore_wait(barrier, NR + NC - 2)
 
     perm_copies = [
-        send(perm.at[LX - 1], plx, perm_s.at[0], perm_r.at[0], up_row, col),
-        send(perm.at[0], phx, perm_s.at[1], perm_r.at[1], down_row, col),
-        send(perm.at[:, pl.ds(LY - 16, 16), :], ply, perm_s.at[2], perm_r.at[2], row, up_col),
-        send(perm.at[:, pl.ds(0, 16), :], phy, perm_s.at[3], perm_r.at[3], row, down_col),
+        send(perm_in.at[LX - 1], plx, perm_s.at[0], perm_r.at[0], up_row, col),
+        send(perm_in.at[0], phx, perm_s.at[1], perm_r.at[1], down_row, col),
+        send(perm_in.at[:, pl.ds(LY - 16, 16), :], ply, perm_s.at[2], perm_r.at[2], row, up_col),
+        send(perm_in.at[:, pl.ds(0, 16), :], phy, perm_s.at[3], perm_r.at[3], row, down_col),
     ]
     for copy in perm_copies:
         copy.start()
@@ -166,7 +170,7 @@
             send(asrc.at[u], acol.at[u, col], ac_s.at[u], ac_r.at[u], row, lax.rem(col + k, NC)).start()
             return carry
 
-        lax.fori_loop(1, NC, step, 0)
+        lax.fori_loop(1, NC, step, 0, unroll=True)
 
     def sums_end(u):
         whole = send(acol.at[u, pl.ds(0, NC - 1)], acol.at[u, pl.ds(0, NC - 1)], ac_s.at[u], ac_r.at[u], row, col)
@@ -180,7 +184,7 @@
             send(bsrc.at[u], arow.at[u, row], ar_s.at[u], ar_r.at[u], lax.rem(row + k, NR), col).start()
             return carry
 
-        lax.fori_loop(1, NR, step, 0)
+        lax.fori_loop(1, NR, step, 0, unroll=True)
         whole = send(arow.at[u, pl.ds(0, NR - 1)], arow.at[u, pl.ds(0, NR - 1)], ar_s.at[u], ar_r.at[u], row, col)
         whole.wait_recv()
         whole.wait_send()
@@ -199,11 +203,11 @@
 
     def first_pass(b, total):
         x, y = lax.div(b, 4), pl.multiple_of(lax.rem(b, 4) * 32, 32)
-        value = rs[x, pl.ds(y, 32), :]
-        res[x, pl.ds(y, 32), :] = value
+        value = res[x, pl.ds(y, 32), :]
         squares = value * value
         return total + (squares[0:8] + squares[8:16]) + (squares[16:24] + squares[24:32])
 
+    loads[0].wait()
     total = lax.fori_loop(0, 16, first_pass, jnp.zeros((8, NZ), F32))
     sums_begin(0, tile_of([total]))
 
@@ -213,11 +217,12 @@
         padp[x + 1, pl.ds(pl.multiple_of(y + 8, 8), 32), :] = value
         logp[x, pl.ds(y, 32), :] = jnp.log(value)
         zero = jnp.zeros((32, NZ), F32)
-        sol[x, pl.ds(y, 32), :] = zero
         prev[x, pl.ds(y, 32), :] = zero
         image[x, pl.ds(y, 32), :] = zero
         return carry
 
+    for copy in loads[1:5]:
+        copy.wait()
     lax.fori_loop(0, 16, second_pass, 0)
     mix_high, mix_low = split(mixv[:, 0:CH] * 0.5)
     rows_iota = lax.broadcasted_iota(jnp.int32, (128, 256), 0)
@@ -226,32 +231,6 @@
     for n, piece in enumerate((mix_high, mix_low)):
         wide = dot(left_map[...], dot(piece, right_map[...]).astype(BF16))
         maps[n * 128 : (n + 1) * 128, :] = jnp.where(same, wide, 0.0).astype(BF16)
-
-    for copy in perm_copies:
-        copy.wait()
-    padp[0, pl.ds(8, LY), :] = plx[...].astype(F32)
-    padp[LX + 1, pl.ds(8, LY), :] = phx[...].astype(F32)
-    for x in range(LX):
-        padp[x + 1, pl.ds(0, 8), :] = ply[x].astype(F32)[8:16]
-        padp[x + 1, pl.ds(LY + 8, 8), :] = phy[x].astype(F32)[0:8]
-
-    @pl.when(row == 0)
-    def _():
-        padp[0, pl.ds(8, LY), :] = padp[1, pl.ds(8, LY), :]
-
-    @pl.when(row == NR - 1)
-    def _():
-        padp[LX + 1, pl.ds(8, LY), :] = padp[LX, pl.ds(8, LY), :]
-
-    @pl.when(col == 0)
-    def _():
-        for x in range(LX):
-            padp[x + 1, pl.ds(0, 8), :] = jnp.broadcast_to(padp[x + 1, pl.ds(8, 8), :][0:1], (8, NZ))
-
-    @pl.when(col == NC - 1)
-    def _():
-        for x in range(LX):
-            padp[x + 1, pl.ds(LY + 8, 8), :] = jnp.broadcast_to(padp[x + 1, pl.ds(LY, 8), :][7:8], (8, NZ))
 
     lanes = lax.broadcasted_iota(jnp.int32, (32, NZ), 1)
 
@@ -270,16 +249,43 @@
             ref[x, pl.ds(pl.multiple_of(y + 8, 8), 32), :], ref[x + 2, pl.ds(pl.multiple_of(y + 8, 8), 32), :], own[7:39], own[9:41], before, after
         )
 
-    def face_pass(b, carry):
-        x, y = lax.div(b, 4), pl.multiple_of(lax.rem(b, 4) * 32, 32)
-        here, others = around(padp, x, y, True)
-        for n, other in enumerate(others):
-            faces[n, x, pl.ds(y, 32), :] = 2.0 * here * other / (here + other)
-        return carry
-
-    lax.fori_loop(0, 16, face_pass, 0)
-
-    for copy in table_copies:
+    def build_faces():
+        for copy in perm_copies:
+            copy.wait()
+        padp[0, pl.ds(8, LY), :] = plx[...].astype(F32)
+        padp[LX + 1, pl.ds(8, LY), :] = phx[...].astype(F32)
+        for x in range(LX):
+            padp[x + 1, pl.ds(0, 8), :] = ply[x].astype(F32)[8:16]
+            padp[x + 1, pl.ds(LY + 8, 8), :] = phy[x].astype(F32)[0:8]
+
+        @pl.when(row == 0)
+        def _():
+            padp[0, pl.ds(8, LY), :] = padp[1, pl.ds(8, LY), :]
+
+        @pl.when(row == NR - 1)
+        def _():
+            padp[LX + 1, pl.ds(8, LY), :] = padp[LX, pl.ds(8, LY), :]
+
+        @pl.when(col == 0)
+        def _():
+            for x in range(LX):
+                padp[x + 1, pl.ds(0, 8), :] = jnp.broadcast_to(padp[x + 1, pl.ds(8, 8), :][0:1], (8, NZ))
+
+        @pl.when(col == NC - 1)
+        def _():
+            for x in range(LX):
+                padp[x + 1, pl.ds(LY + 8, 8), :] = jnp.broadcast_to(padp[x + 1, pl.ds(LY, 8), :][7:8], (8, NZ))
+
+        def face_pass(b, carry):
+            x, y = lax.div(b, 4), pl.multiple_of(lax.rem(b, 4) * 32, 32)
+            here, others = around(padp, x, y, True)
+            for n, other in enumerate(others):
+                faces[n, x, pl.ds(y, 32), :] = 2.0 * here * other / (here + other)
+            return carry
+
+        lax.fori_loop(0, 16, face_pass, 0)
+
+    for copy in loads[5:]:
         copy.wait()
     state[0] = jnp.broadcast_to(sums_end(0)[0:1], (8, 128))
     state[1] = jnp.ones((8, 128), F32)
@@ -293,6 +299,24 @@
         mean = state[0][0:1, 0:1] * (1.0 / CELLS) + 1e-6
         scale = jnp.sqrt(mean)
         inverse = 1.0 / scale
+
+        def along_x(cq):
+            whole = send(
+                sf.at[cq, pl.ds(0, NR - 1)], vf.at[cq, pl.ds(0, NR - 1)], f_s.at[cq], f_r.at[cq], row, col
+            )
+            whole.wait_recv()
+            whole.wait_send()
+            high, low = split(vf[cq].reshape(256, 128))
+            both = dot(xt[...], high)
+            sx[cq] = (both[:64] + both[64:] + dot(xt[0:64, :], low)).reshape(NC, 8, 128)
+            vx[cq, col] = sx[cq, col]
+
+            def scatter(k, carry):
+                to = lax.rem(col + k, NC)
+                send(sx.at[cq, to], vx.at[cq, col], x_s.at[cq], x_r.at[cq], row, to).start()
+                return carry
+
+            lax.fori_loop(1, NC, scatter, 0, unroll=True)
 
         def forward(cq, carry):
             def lift_pass(b, carry):
@@ -301,14 +325,14 @@
                 logs = logp[x, pl.ds(y, 8), :]
                 for c4 in range(4):
                     c = cq * 4 + c4
-                    half = (lw[c, 0] * 0.5) * scaled + (lw[c, 1] * 0.5) * logs + lw[c, 2] * 0.5
+                    half = (lw[0, c] * 0.5) * scaled + (lw[1, c] * 0.5) * logs + lw[2, c] * 0.5
                     inner = half * (2.0 * GELU_A + (8.0 * 0.044715 * GELU_A) * (half * half))
                     value = half + half * jnp.tanh(inner)
                     rest = value - value.astype(BF16).astype(F32)
                     lift[b, c] = jnp.concatenate([value, rest], axis=0).astype(BF16)
                 return carry
 
-            lax.fori_loop(0, 64, lift_pass, 0)
+            lax.fori_loop(0, 64, lift_pass, 0, unroll=8)
             tops, bottoms = [], []
             for c4 in range(4):
                 c = cq * 4 + c4
@@ -324,11 +348,13 @@
             )
             both = dot(yt[...], high)
             flat = both[:64] + both[64:] + dot(yt[0:64, :], low)
+            turned = []
             for ri in range(2):
                 square = jnp.concatenate(
                     [flat[ri * 32 : ri * 32 + 32, c4 * 128 : c4 * 128 + 128] for c4 in range(4)], axis=0
                 )
-                sf[cq, :, pl.ds(ri * 8, 8), :] = square.T.reshape(NR, 8, 128)
+                turned.append(square.T.reshape(NR, 8, 128))
+            sf[cq] = jnp.concatenate(turned, axis=1)
             vf[cq, row] = sf[cq, row]
 
             def step(k, carry):
@@ -336,43 +362,27 @@
                 send(sf.at[cq, to], vf.at[cq, row], f_s.at[cq], f_r.at[cq], to, col).start()
                 return carry
 
-            lax.fori_loop(1, NR, step, 0)
+            lax.fori_loop(1, NR, step, 0, unroll=True)
+
             return carry
 
         lax.fori_loop(0, 4, forward, 0)
-
-        def point_pass(b, carry):
-            x, y = lax.div(b, 16), lax.rem(b, 16)
-            both = dot(maps[...], lift[b].reshape(256, NZ))
-            point[x, y] = (both[:128] + both[128:]).reshape(CH, 8, NZ)
-            return carry
-
-        lax.fori_loop(0, 64, point_pass, 0)
-
-        blocks = []
+        for cq in range(4):
+            along_x(cq)
+
+        @pl.when(i == 0)
+        def _():
+            build_faces()
+
+
+        spectrum = []
         for cq in range(4):
             whole = send(
-                sf.at[cq, pl.ds(0, NR - 1)], vf.at[cq, pl.ds(0, NR - 1)], f_s.at[cq], f_r.at[cq], row, col
+                sx.at[cq, pl.ds(0, NC - 1)], vx.at[cq, pl.ds(0, NC - 1)], x_s.at[cq], x_r.at[cq], row, col
             )
             whole.wait_recv()
             whole.wait_send()
-            blocks.append(vf[cq].reshape(256, 128))
-        high, low = split(jnp.concatenate(blocks, axis=1))
-        both = dot(xt[...], high)
-        partial = both[:64] + both[64:] + dot(xt[0:64, :], low)
-        sx[...] = partial.reshape(NC, 8, 512)
-        vx[col] = sx[col]
-
-        def scatter(k, carry):
-            to = lax.rem(col + k, NC)
-            send(sx.at[to], vx.at[col], x_s, x_r, row, to).start()
-            return carry
-
-        lax.fori_loop(1, NC, scatter, 0)
-        whole = send(sx.at[pl.ds(0, NC - 1)], vx.at[pl.ds(0, NC - 1)], x_s, x_r, row, col)
-        whole.wait_recv()
-        whole.wait_send()
-        spectrum = jnp.sum(vx[...], axis=0)
+            spectrum.append(jnp.sum(vx[cq], axis=0))
 
         stacks = []
         for ri in range(2):
@@ -380,7 +390,7 @@
             for r in range(4):
                 line = r * 2 + ri
                 wide = [
-                    jnp.broadcast_to(spectrum[line : line + 1, q * 128 : q * 128 + 128], (8, 128)) for q in range(4)
+                    jnp.broadcast_to(spectrum[q][line : line + 1], (8, 128)) for q in range(4)
                 ]
                 tall = jnp.concatenate(
                     [jnp.where(low_half, wide[0], wide[1]), jnp.where(low_half, wide[2], wide[3])], axis=0
@@ -422,7 +432,7 @@
             send(sm, vm.at[col], m_s, m_r, row, lax.rem(col + k, NC)).start()
             return carry
 
-        lax.fori_loop(1, NC, spread_out, 0)
+        lax.fori_loop(1, NC, spread_out, 0, unroll=True)
         whole = send(vm.at[pl.ds(0, NC - 1)], vm.at[pl.ds(0, NC - 1)], m_s, m_r, row, col)
         whole.wait_recv()
         whole.wait_send()
@@ -438,7 +448,15 @@
                 send(sh.at[oq, to], vh.at[oq, row], h_s.at[oq], h_r.at[oq], to, col).start()
                 return carry
 
-            lax.fori_loop(1, NR, step, 0)
+            lax.fori_loop(1, NR, step, 0, unroll=True)
+
+        def point_pass(b, carry):
+            x, y = lax.div(b, 16), lax.rem(b, 16)
+            both = dot(maps[...], lift[b].reshape(256, NZ))
+            point[x, y] = (both[:128] + both[128:]).reshape(CH, 8, NZ)
+            return carry
+
+        lax.fori_loop(0, 64, point_pass, 0, unroll=8)
 
         def clear(b, carry):
             x, y = lax.div(b, 4), pl.multiple_of(lax.rem(b, 4) * 32, 32)
@@ -466,31 +484,29 @@
             for o4 in range(4):
                 part = back[:, o4 * 128 : o4 * 128 + 128]
                 high, low = split(jnp.concatenate([part[:128], part[128:]], axis=1))
-                modes[o4] = jnp.concatenate([high, low, high], axis=1)
-
-            for x in range(LX):
-                for o4 in range(4):
-                    o = oq * 4 + o4
-                    bias = mw[o, CH] * 0.5
-                    weight_out = pw[o]
-                    wave = dot(modes[o4], ti[:, x * NZ : x * NZ + NZ])
-                    half = wave + point[x, :, o].reshape(128, NZ) + bias
-                    inner = half * (2.0 * GELU_A + (8.0 * 0.044715 * GELU_A) * (half * half))
-                    hidden = weight_out * (half + half * jnp.tanh(inner))
-                    padk[x + 1, pl.ds(8, LY), :] += hidden
+                modes[oq * 4 + o4] = jnp.concatenate([high, low, high], axis=1)
             return carry
 
         lax.fori_loop(0, 4, backward, 0)
 
-        def finish(b, carry):
-            x, y = lax.div(b, 4), pl.multiple_of(lax.rem(b, 4) * 32, 32)
-            value = scale * padk[x + 1, pl.ds(pl.multiple_of(y + 8, 8), 32), :]
-            padk[x + 1, pl.ds(pl.multiple_of(y + 8, 8), 32), :] = value
-            kept[i, x, pl.ds(y, 32), :] = value
-            return carry
-
-        lax.fori_loop(0, 16, finish, 0)
-
+        def planes(xs):
+            def channels(oq, carry):
+                for x in xs:
+                    for o4 in range(4):
+                        o = oq * 4 + o4
+                        bias = mw[o, CH] * 0.5
+                        wave = dot(modes[o], ti[x])
+                        half = wave + point[x, :, o].reshape(LY, NZ) + bias
+                        inner = half * (2.0 * GELU_A + (8.0 * 0.044715 * GELU_A) * (half * half))
+                        hidden = pw[o] * (half + half * jnp.tanh(inner))
+                        padk[x + 1, pl.ds(8, LY), :] += hidden
+                return carry
+
+            lax.fori_loop(0, 4, channels, 0)
+            for x in xs:
+                padk[x + 1, pl.ds(8, LY), :] = scale * padk[x + 1, pl.ds(8, LY), :]
+
+        planes((0, LX - 1))
         copies = [
             send(padk.at[LX, pl.ds(8, LY)], padk.at[0, pl.ds(8, LY)], halo_s.at[0], halo_r.at[0], up_row, col),
             send(padk.at[1, pl.ds(8, LY)], padk.at[LX + 1, pl.ds(8, LY)], halo_s.at[1], halo_r.at[1], down_row, col),
@@ -503,8 +519,13 @@
                 halo_s.at[3], halo_r.at[3], row, down_col,
             ),
         ]
-        for copy in copies:
+        for copy in copies[:2]:
             copy.start()
+        planes(range(1, LX - 1))
+        for copy in copies[2:]:
+            copy.start()
+        keep = pltpu.make_async_copy(padk.at[pl.ds(1, LX), pl.ds(8, LY)], kept_out.at[i], kept_s)
+        keep.start()
         for copy in copies:
             copy.wait()
 
@@ -552,18 +573,26 @@
         curve = k_ak - 2.0 * beta * k_img + beta * beta * old_curve
         alpha = (r_k - beta * r_d) / curve
 
-        def update(b, carry):
-            x, y = lax.div(b, 4), pl.multiple_of(lax.rem(b, 4) * 32, 32)
-            at = (x, pl.ds(y, 32), slice(None))
-            direction = padk[x + 1, pl.ds(pl.multiple_of(y + 8, 8), 32), :] - beta * prev[at]
-            applied = fresh[at] - beta * image[at]
-            prev[at] = direction
-            image[at] = applied
-            sol[at] = sol[at] + alpha * direction
-            res[at] = res[at] - alpha * applied
-            return carry
-
-        lax.fori_loop(0, 16, update, 0)
+        show = pltpu.make_async_copy(fresh, image_out.at[i], image_s)
+        show.start()
+
+        @pl.when(i == 0)
+        def _():
+            def update(b, carry):
+                x, y = lax.div(b, 4), pl.multiple_of(lax.rem(b, 4) * 32, 32)
+                at = (x, pl.ds(y, 32), slice(None))
+                applied = fresh[at]
+                prev[at] = padk[x + 1, pl.ds(pl.multiple_of(y + 8, 8), 32), :]
+                image[at] = applied
+                res[at] = res[at] - alpha * applied
+                return carry
+
+            lax.fori_loop(0, 16, update, 0)
+
+        steps_out[i] = jnp.broadcast_to(alpha, (8, 128))
+        steps_out[2 + i] = jnp.broadcast_to(beta, (8, 128))
+        keep.wait()
+        show.wait()
         squares = state[0][0:1, 0:1] - 2.0 * alpha * r_ak + alpha * alpha * ak_ak
         state[0] = jnp.broadcast_to(jnp.maximum(squares, 0.0), (8, 128))
         state[1] = jnp.broadcast_to(curve, (8, 128))
@@ -572,13 +601,33 @@
     lax.fori_loop(0, 2, iteration, 0)
 
 
+def last(steps, rs, kept_in, image_in, sol_out, res_out, kept_out):
+    first, second = steps[0, 0:1, 0:1], steps[1, 0:1, 0:1]
+    first = first - second * steps[3, 0:1, 0:1]
+    sol_out[0] = first * kept_in[0, 0] + second * kept_in[1, 0]
+    res_out[0] = rs[0] - (first * image_in[0, 0] + second * image_in[1, 0])
+    kept_out[...] = kept_in[...]
+
+
 def local(right_side, permeability, lift_weight, spectral_weight, mix_weight, proj_weight):
-    vmem = pl.BlockSpec(memory_space=pltpu.VMEM)
     smem = pl.BlockSpec(memory_space=pltpu.SMEM)
     hbm = pl.BlockSpec(memory_space=pl.ANY)
     field = (LX, LY, NZ)
     dma = pltpu.SemaphoreType.DMA
     scratch = [
+        pltpu.VMEM(field, F32),
+        pltpu.VMEM(field, BF16),
+        pltpu.VMEM((CH, CH + 1), F32),
+        pltpu.VMEM((2, 2, CH, CH, 64), F32),
+        pltpu.VMEM((LX * NZ, 256), BF16),
+        pltpu.VMEM((LX, 768, NZ), BF16),
+        pltpu.VMEM((128, 256), BF16),
+        pltpu.VMEM((256, 192), BF16),
+        pltpu.VMEM((512, 128), BF16),
+        pltpu.VMEM((128, 512), BF16),
+        pltpu.VMEM((32, 128), BF16),
+        pltpu.VMEM((128, 16), BF16),
+        pltpu.VMEM((16, 256), BF16),
         pltpu.VMEM((64, CH, 16, NZ), BF16),
         pltpu.VMEM((LX, 16, CH, 8, NZ), F32),
         pltpu.VMEM(field, F32),
@@ -597,40 +646,47 @@
         pltpu.VMEM((LX, 16, NZ), BF16),
         pltpu.VMEM((4, NR, 16, 128), F32),
         pltpu.VMEM((4, NR, 16, 128), F32),
-        pltpu.VMEM((NC, 8, 512), F32),
-        pltpu.VMEM((NC, 8, 512), F32),
+        pltpu.VMEM((4, NC, 8, 128), F32),
+        pltpu.VMEM((4, NC, 8, 128), F32),
         pltpu.VMEM((4, 8, 128), F32),
         pltpu.VMEM((NC, 4, 8, 128), F32),
         pltpu.VMEM((4, NR, 16, 128), F32),
         pltpu.VMEM((4, NR, 16, 128), F32),
-        pltpu.VMEM((4, LY, 768), BF16),
+        pltpu.VMEM((CH, LY, 768), BF16),
         pltpu.VMEM((3, 8, 128), F32),
         pltpu.VMEM((3, NC, 8, 128), F32),
         pltpu.VMEM((3, 8, 128), F32),
         pltpu.VMEM((3, NR, 8, 128), F32),
         pltpu.VMEM((2, 8, 128), F32),
         dma((4,)), dma((4,)), dma((4,)), dma((4,)), dma((4,)), dma((4,)),
-        dma, dma, dma, dma, dma((4,)), dma((4,)),
-        dma((3,)), dma((3,)), dma((3,)), dma((3,)), dma((2,)),
+        dma((4,)), dma((4,)), dma, dma, dma((4,)), dma((4,)),
+        dma((3,)), dma((3,)), dma((3,)), dma((3,)), dma((15,)), dma, dma,
     ]
     constants = [jnp.asarray(t) for t in tables()]
-    return pl.pallas_call(
+    pair = jax.ShapeDtypeStruct((2,) + field, F32)
+    kept, images, steps = pl.pallas_call(
         kernel,
-        out_shape=[
-            jax.ShapeDtypeStruct(field, F32),
-            jax.ShapeDtypeStruct(field, F32),
-            jax.ShapeDtypeStruct((2,) + field, F32),
-        ],
-        in_specs=[vmem, vmem, smem, smem, smem, vmem, vmem, vmem, vmem, hbm, hbm] + [vmem] * 7,
-        out_specs=[vmem, vmem, vmem],
+        out_shape=[pair, pair, jax.ShapeDtypeStruct((4, 8, 128), F32)],
+        in_specs=[hbm, hbm, smem, smem, smem] + [hbm] * 13,
+        out_specs=[hbm, hbm, pl.BlockSpec(memory_space=pltpu.VMEM)],
         scratch_shapes=scratch,
         compiler_params=pltpu.CompilerParams(
             collective_id=0, has_side_effects=True, vmem_limit_bytes=56 * 1024 * 1024
         ),
     )(
-        right_side, permeability, lift_weight, mix_weight, proj_weight, mix_weight,
+        right_side, permeability, lift_weight.T, mix_weight, proj_weight, mix_weight,
         spectral_weight, *constants,
     )
+    plane = (1, LY, NZ)
+    one = pl.BlockSpec(plane, lambda x: (x, 0, 0))
+    two = pl.BlockSpec((2,) + plane, lambda x: (0, x, 0, 0))
+    return pl.pallas_call(
+        last,
+        grid=(LX,),
+        out_shape=[jax.ShapeDtypeStruct(field, F32), jax.ShapeDtypeStruct(field, F32), pair],
+        in_specs=[pl.BlockSpec((4, 8, 128), lambda x: (0, 0, 0)), one, two, two],
+        out_specs=[one, one, two],
+    )(steps, right_side, kept, images)
 
 
 def solution(mesh):

time: 170 us -> 128 us (0.75)
  Pallas kernels: 163 us -> 127 us
  local copies, waits for them, and re-layouts: 6.15 us -> 0 us
    pallas_call x1 -> x2, Pallas kernels: 163 us -> 127 us  [the longest x1 123 us: local(): pl.pallas_call(kernel, out_shape=[pair, pair, jax.ShapeDtypeStruct((4, 8,...]
    unnamed x6 -> x0, local copies, waits for them, and re-layouts: 6.15 us -> none
where the time goes in v2:
time: 128 us; the launch traced here: 127 us
  Pallas kernels  127 us (99%)
    pallas_call x1, Pallas kernels, local(): pl.pallas_call(kernel, out_shape=[pair, pair, jax.ShapeDtypeStruct((4, 8,...  123 us
    pallas_call x1, Pallas kernels, local(): pl.pallas_call(last, grid=(LX,), out_shape=[jax.ShapeDtypeStruct(field, F...  3.93 us

profile of v2, /device:TPU:1, one launch (start us, length us, event | category | flops | bytes accessed | tf_op | source)
XLA Modules:
  0.0 127.4 jit_solution(12876486076124510890)
XLA Ops:
  0.6 122.9 %shard_map.184 = (f32[2,4,128,256]{3,2,1,0:T(8,128)}, f32[2,4,128,256]{3,2,1,0:T(8,128)}, f32[4,8,128]{2,1,0:T(8,128)}) custom-call(f32[4,128,256]{2,1,0:T(8,128)} %rs.3, bf16[4,128,256]{2,1,0:T(8,128)(2,1)} %perm_in.1, f32[3,16]{1,0:T(4,128)} %bitcast.1, f32[16,17]{1,0:T(8,128)} %mix_in.1, f32[17]{0:T(128)} %pw.1, f32[16,17]{1,0:T(8,128)} %mix_in.1, ...), custom_call_target="tpu_custom_call" | custom-call | tf_op jit(solution)/shard_map/pallas_call | solution.py:667
  123.5 3.9 %shard_map.185 = (f32[4,128,256]{2,1,0:T(8,128)}, f32[4,128,256]{2,1,0:T(8,128)}, f32[2,4,128,256]{3,2,1,0:T(8,128)}) custom-call(f32[4,8,128]{2,1,0:T(8,128)} %get-tuple-element.6.steps, f32[4,128,256]{2,1,0:T(8,128)} %rs.3, f32[2,4,128,256]{3,2,1,0:T(8,128)} %get-tuple-element.7.kept_in, f32[2,4,128,256]{3,2,1,0:T(8,128)} %get-tuple-element.8.image_in), custom_call_target="tpu_custom_call" | custom-call | tf_op jit(solution)/shard_map/pallas_call | solution.py:683

commit v3 on v2

--- a/solution.py
+++ b/solution.py
@@ -117,8 +117,8 @@
     lift, point, logp, padk, padp, faces, prev, image, fresh, maps, yt, yi,
     plx, phx, ply, phy,
     sf, vf, sx, vx, sm, vm, sh, vh, modes,
-    asrc, acol, bsrc, arow, state,
-    perm_s, perm_r, halo_s, halo_r, f_s, f_r, x_s, x_r, m_s, m_r, h_s, h_r, ac_s, ac_r, ar_s, ar_r, table_s, kept_s, image_s,
+    asrc, aall, state,
+    perm_s, perm_r, halo_s, halo_r, f_s, f_r, x_s, x_r, m_s, m_r, h_s, h_r, ac_s, ac_r, table_s, kept_s, image_s,
 ):
     row = lax.axis_index("row")
     col = lax.axis_index("col")
@@ -141,17 +141,20 @@
 
     barrier = pltpu.get_barrier_semaphore()
 
-    def greet_row(k, carry):
-        pl.semaphore_signal(barrier, 1, device_id=(lax.rem(row + k, NR), col), device_id_type=MESH)
-        return carry
-
-    def greet_col(k, carry):
-        pl.semaphore_signal(barrier, 1, device_id=(row, lax.rem(col + k, NC)), device_id_type=MESH)
-        return carry
-
-    lax.fori_loop(1, NR, greet_row, 0, unroll=True)
-    lax.fori_loop(1, NC, greet_col, 0, unroll=True)
-    pl.semaphore_wait(barrier, NR + NC - 2)
+    def to_all(act):
+        for other in range(1, NC):
+            act(row, lax.rem(col + other, NC))
+
+        def step(k, carry):
+            to_row = lax.rem(row + k, NR)
+            for other in range(NC):
+                act(to_row, lax.rem(col + other, NC))
+            return carry
+
+        lax.fori_loop(1, NR, step, 0)
+
+    to_all(lambda r, c: pl.semaphore_signal(barrier, 1, device_id=(r, c), device_id_type=MESH))
+    pl.semaphore_wait(barrier, NR * NC - 1)
 
     perm_copies = [
         send(perm_in.at[LX - 1], plx, perm_s.at[0], perm_r.at[0], up_row, col),
@@ -162,33 +165,19 @@
     for copy in perm_copies:
         copy.start()
 
-    def sums_begin(u, tile):
-        asrc[u] = tile
-        acol[u, col] = tile
-
-        def step(k, carry):
-            send(asrc.at[u], acol.at[u, col], ac_s.at[u], ac_r.at[u], row, lax.rem(col + k, NC)).start()
-            return carry
-
-        lax.fori_loop(1, NC, step, 0, unroll=True)
+    def sums_begin(u, line):
+        me = row * NC + col
+        asrc[u] = line
+        aall[u, me] = line
+        to_all(lambda r, c: send(asrc.at[u], aall.at[u, me], ac_s.at[u], ac_r.at[u], r, c).start())
 
     def sums_end(u):
-        whole = send(acol.at[u, pl.ds(0, NC - 1)], acol.at[u, pl.ds(0, NC - 1)], ac_s.at[u], ac_r.at[u], row, col)
+        whole = send(
+            aall.at[u, pl.ds(0, NR * NC - 1)], aall.at[u, pl.ds(0, NR * NC - 1)], ac_s.at[u], ac_r.at[u], row, col
+        )
         whole.wait_recv()
         whole.wait_send()
-        tile = jnp.sum(acol[u], axis=0)
-        bsrc[u] = tile
-        arow[u, row] = tile
-
-        def step(k, carry):
-            send(bsrc.at[u], arow.at[u, row], ar_s.at[u], ar_r.at[u], lax.rem(row + k, NR), col).start()
-            return carry
-
-        lax.fori_loop(1, NR, step, 0, unroll=True)
-        whole = send(arow.at[u, pl.ds(0, NR - 1)], arow.at[u, pl.ds(0, NR - 1)], ar_s.at[u], ar_r.at[u], row, col)
-        whole.wait_recv()
-        whole.wait_send()
-        return jnp.sum(jnp.sum(arow[u], axis=0), axis=1, keepdims=True)
+        return jnp.sum(aall[u], axis=0)
 
     def tile_of(parts):
         rows = []
@@ -199,7 +188,9 @@
         tile = jnp.zeros((8, 128), F32)
         for i, line in enumerate(rows):
             tile = jnp.where(index == i, jnp.broadcast_to(line, (8, 128)), tile)
-        return tile
+        each = jnp.broadcast_to(jnp.sum(tile, axis=1, keepdims=True), (8, 128))
+        lane = lax.broadcasted_iota(jnp.int32, (8, 128), 1)
+        return jnp.sum(jnp.where(index == lane, each, 0.0), axis=0, keepdims=True)
 
     def first_pass(b, total):
         x, y = lax.div(b, 4), pl.multiple_of(lax.rem(b, 4) * 32, 32)
@@ -287,7 +278,7 @@
 
     for copy in loads[5:]:
         copy.wait()
-    state[0] = jnp.broadcast_to(sums_end(0)[0:1], (8, 128))
+    state[0] = jnp.broadcast_to(sums_end(0)[:, 0:1], (8, 128))
     state[1] = jnp.ones((8, 128), F32)
 
     mask_rows = lax.broadcasted_iota(jnp.int32, (16, 128), 0)
@@ -367,8 +358,18 @@
             return carry
 
         lax.fori_loop(0, 4, forward, 0)
-        for cq in range(4):
-            along_x(cq)
+        def point_pass(b, carry):
+            x, y = lax.div(b, 16), lax.rem(b, 16)
+            both = dot(maps[...], lift[b].reshape(256, NZ))
+            point[x, y] = (both[:128] + both[128:]).reshape(CH, 8, NZ)
+            return carry
+
+        along_x(0)
+        along_x(1)
+        lax.fori_loop(0, 40, point_pass, 0, unroll=8)
+        along_x(2)
+        along_x(3)
+        lax.fori_loop(40, 64, point_pass, 0, unroll=8)
 
         @pl.when(i == 0)
         def _():
@@ -450,14 +451,6 @@
 
             lax.fori_loop(1, NR, step, 0, unroll=True)
 
-        def point_pass(b, carry):
-            x, y = lax.div(b, 16), lax.rem(b, 16)
-            both = dot(maps[...], lift[b].reshape(256, NZ))
-            point[x, y] = (both[:128] + both[128:]).reshape(CH, 8, NZ)
-            return carry
-
-        lax.fori_loop(0, 64, point_pass, 0, unroll=8)
-
         def clear(b, carry):
             x, y = lax.div(b, 4), pl.multiple_of(lax.rem(b, 4) * 32, 32)
             padk[x + 1, pl.ds(pl.multiple_of(y + 8, 8), 32), :] = jnp.full((32, NZ), pw[CH], F32)
@@ -465,7 +458,7 @@
 
         lax.fori_loop(0, 16, clear, 0)
 
-        def backward(oq, carry):
+        def turn(oq):
             whole = send(
                 sh.at[oq, pl.ds(0, NR - 1)], vh.at[oq, pl.ds(0, NR - 1)], h_s.at[oq], h_r.at[oq], row, col
             )
@@ -484,28 +477,31 @@
             for o4 in range(4):
                 part = back[:, o4 * 128 : o4 * 128 + 128]
                 high, low = split(jnp.concatenate([part[:128], part[128:]], axis=1))
-                modes[oq * 4 + o4] = jnp.concatenate([high, low, high], axis=1)
+                modes[o4] = jnp.concatenate([high, low, high], axis=1)
+
+        def channels(oq, xs):
+            for x in xs:
+                for o4 in range(4):
+                    o = oq * 4 + o4
+                    bias = mw[o, CH] * 0.5
+                    wave = dot(modes[o4], ti[x])
+                    half = wave + point[x, :, o].reshape(LY, NZ) + bias
+                    inner = half * (2.0 * GELU_A + (8.0 * 0.044715 * GELU_A) * (half * half))
+                    hidden = pw[o] * (half + half * jnp.tanh(inner))
+                    padk[x + 1, pl.ds(8, LY), :] += hidden
+
+        def backward(oq, carry):
+            turn(oq)
+            channels(oq, range(LX))
             return carry
 
-        lax.fori_loop(0, 4, backward, 0)
-
         def planes(xs):
-            def channels(oq, carry):
-                for x in xs:
-                    for o4 in range(4):
-                        o = oq * 4 + o4
-                        bias = mw[o, CH] * 0.5
-                        wave = dot(modes[o], ti[x])
-                        half = wave + point[x, :, o].reshape(LY, NZ) + bias
-                        inner = half * (2.0 * GELU_A + (8.0 * 0.044715 * GELU_A) * (half * half))
-                        hidden = pw[o] * (half + half * jnp.tanh(inner))
-                        padk[x + 1, pl.ds(8, LY), :] += hidden
-                return carry
-
-            lax.fori_loop(0, 4, channels, 0)
+            channels(3, xs)
             for x in xs:
                 padk[x + 1, pl.ds(8, LY), :] = scale * padk[x + 1, pl.ds(8, LY), :]
 
+        lax.fori_loop(0, 3, backward, 0)
+        turn(3)
         planes((0, LX - 1))
         copies = [
             send(padk.at[LX, pl.ds(8, LY)], padk.at[0, pl.ds(8, LY)], halo_s.at[0], halo_r.at[0], up_row, col),
@@ -567,7 +563,7 @@
         totals = lax.fori_loop(0, 16, operator_pass, tuple(jnp.zeros((8, NZ), F32) for _ in range(6)))
         sums_begin(1 + i, tile_of(totals))
         sums = sums_end(1 + i)
-        k_ak, k_img, r_k, r_d, r_ak, ak_ak = [sums[n : n + 1] for n in range(6)]
+        k_ak, k_img, r_k, r_d, r_ak, ak_ak = [sums[:, n : n + 1] for n in range(6)]
         old_curve = state[1][0:1, 0:1]
         beta = k_img / old_curve
         curve = k_ak - 2.0 * beta * k_img + beta * beta * old_curve
@@ -604,8 +600,8 @@
 def last(steps, rs, kept_in, image_in, sol_out, res_out, kept_out):
     first, second = steps[0, 0:1, 0:1], steps[1, 0:1, 0:1]
     first = first - second * steps[3, 0:1, 0:1]
-    sol_out[0] = first * kept_in[0, 0] + second * kept_in[1, 0]
-    res_out[0] = rs[0] - (first * image_in[0, 0] + second * image_in[1, 0])
+    sol_out[...] = first * kept_in[0] + second * kept_in[1]
+    res_out[...] = rs[...] - (first * image_in[0] + second * image_in[1])
     kept_out[...] = kept_in[...]
 
 
@@ -652,15 +648,13 @@
         pltpu.VMEM((NC, 4, 8, 128), F32),
         pltpu.VMEM((4, NR, 16, 128), F32),
         pltpu.VMEM((4, NR, 16, 128), F32),
-        pltpu.VMEM((CH, LY, 768), BF16),
-        pltpu.VMEM((3, 8, 128), F32),
-        pltpu.VMEM((3, NC, 8, 128), F32),
-        pltpu.VMEM((3, 8, 128), F32),
-        pltpu.VMEM((3, NR, 8, 128), F32),
+        pltpu.VMEM((4, LY, 768), BF16),
+        pltpu.VMEM((3, 1, 128), F32),
+        pltpu.VMEM((3, NR * NC, 1, 128), F32),
         pltpu.VMEM((2, 8, 128), F32),
         dma((4,)), dma((4,)), dma((4,)), dma((4,)), dma((4,)), dma((4,)),
         dma((4,)), dma((4,)), dma, dma, dma((4,)), dma((4,)),
-        dma((3,)), dma((3,)), dma((3,)), dma((3,)), dma((15,)), dma, dma,
+        dma((3,)), dma((3,)), dma((15,)), dma, dma,
     ]
     constants = [jnp.asarray(t) for t in tables()]
     pair = jax.ShapeDtypeStruct((2,) + field, F32)
@@ -677,12 +671,12 @@
         right_side, permeability, lift_weight.T, mix_weight, proj_weight, mix_weight,
         spectral_weight, *constants,
     )
-    plane = (1, LY, NZ)
+    plane = (2, LY, NZ)
     one = pl.BlockSpec(plane, lambda x: (x, 0, 0))
     two = pl.BlockSpec((2,) + plane, lambda x: (0, x, 0, 0))
     return pl.pallas_call(
         last,
-        grid=(LX,),
+        grid=(LX // 2,),
         out_shape=[jax.ShapeDtypeStruct(field, F32), jax.ShapeDtypeStruct(field, F32), pair],
         in_specs=[pl.BlockSpec((4, 8, 128), lambda x: (0, 0, 0)), one, two, two],
         out_specs=[one, one, two],

time: 128 us -> 120 us (0.938)
  Pallas kernels: 127 us -> 120 us
    pallas_call x1, Pallas kernels: 123 us -> 117 us  [local(): pl.pallas_call(kernel, out_shape=[pair, pair, jax.ShapeDtypeStruct((4, 8,...]
where the time goes in v3:
time: 120 us
  Pallas kernels  120 us (100%)
    pallas_call x1, Pallas kernels, local(): pl.pallas_call(kernel, out_shape=[pair, pair, jax.ShapeDtypeStruct((4, 8,...  117 us
    pallas_call x1, Pallas kernels, local(): pl.pallas_call(last, grid=(LX // 2,), out_shape=[jax.ShapeDtypeStruct(fie...  2.83 us

profile of v3, /device:TPU:1, one launch (start us, length us, event | category | flops | bytes accessed | tf_op | source)
XLA Modules:
  0.0 120.3 jit_solution(9997335580321776317)
XLA Ops:
  0.6 116.8 %shard_map.184 = (f32[2,4,128,256]{3,2,1,0:T(8,128)}, f32[2,4,128,256]{3,2,1,0:T(8,128)}, f32[4,8,128]{2,1,0:T(8,128)}) custom-call(f32[4,128,256]{2,1,0:T(8,128)} %rs.3, bf16[4,128,256]{2,1,0:T(8,128)(2,1)} %perm_in.1, f32[3,16]{1,0:T(4,128)} %bitcast.1, f32[16,17]{1,0:T(8,128)} %mix_in.1, f32[17]{0:T(128)} %pw.1, f32[16,17]{1,0:T(8,128)} %mix_in.1, ...), custom_call_target="tpu_custom_call" | custom-call | tf_op jit(solution)/shard_map/pallas_call | solution.py:661
  117.4 2.8 %shard_map.185 = (f32[4,128,256]{2,1,0:T(8,128)}, f32[4,128,256]{2,1,0:T(8,128)}, f32[2,4,128,256]{3,2,1,0:T(8,128)}) custom-call(f32[4,8,128]{2,1,0:T(8,128)} %get-tuple-element.6.steps, f32[4,128,256]{2,1,0:T(8,128)} %rs.3, f32[2,4,128,256]{3,2,1,0:T(8,128)} %get-tuple-element.7.kept_in, f32[2,4,128,256]{3,2,1,0:T(8,128)} %get-tuple-element.8.image_in), custom_call_target="tpu_custom_call" | custom-call | tf_op jit(solution)/shard_map/pallas_call | solution.py:677

commit v4 on v3

--- a/solution.py
+++ b/solution.py
@@ -199,7 +199,7 @@
         return total + (squares[0:8] + squares[8:16]) + (squares[16:24] + squares[24:32])
 
     loads[0].wait()
-    total = lax.fori_loop(0, 16, first_pass, jnp.zeros((8, NZ), F32))
+    total = lax.fori_loop(0, 16, first_pass, jnp.zeros((8, NZ), F32), unroll=4)
     sums_begin(0, tile_of([total]))
 
     def second_pass(b, carry):
@@ -310,20 +310,24 @@
             lax.fori_loop(1, NC, scatter, 0, unroll=True)
 
         def forward(cq, carry):
+            factors = [
+                [jnp.full((8, NZ), lw[k, cq * 4 + c4] * 0.5, F32) for k in range(3)] for c4 in range(4)
+            ]
+
             def lift_pass(b, carry):
                 x, y = lax.div(b, 16), pl.multiple_of(lax.rem(b, 16) * 8, 8)
                 scaled = res[x, pl.ds(y, 8), :] * inverse
                 logs = logp[x, pl.ds(y, 8), :]
                 for c4 in range(4):
                     c = cq * 4 + c4
-                    half = (lw[0, c] * 0.5) * scaled + (lw[1, c] * 0.5) * logs + lw[2, c] * 0.5
+                    half = factors[c4][0] * scaled + factors[c4][1] * logs + factors[c4][2]
                     inner = half * (2.0 * GELU_A + (8.0 * 0.044715 * GELU_A) * (half * half))
                     value = half + half * jnp.tanh(inner)
                     rest = value - value.astype(BF16).astype(F32)
                     lift[b, c] = jnp.concatenate([value, rest], axis=0).astype(BF16)
                 return carry
 
-            lax.fori_loop(0, 64, lift_pass, 0, unroll=8)
+            lax.fori_loop(0, 64, lift_pass, 0, unroll=16)
             tops, bottoms = [], []
             for c4 in range(4):
                 c = cq * 4 + c4
@@ -560,17 +564,16 @@
             )
             return tuple(total + fold8(term) for total, term in zip(totals, terms))
 
-        totals = lax.fori_loop(0, 16, operator_pass, tuple(jnp.zeros((8, NZ), F32) for _ in range(6)))
+        totals = lax.fori_loop(0, 16, operator_pass, tuple(jnp.zeros((8, NZ), F32) for _ in range(6)), unroll=2)
         sums_begin(1 + i, tile_of(totals))
+        show = pltpu.make_async_copy(fresh, image_out.at[i], image_s)
+        show.start()
         sums = sums_end(1 + i)
         k_ak, k_img, r_k, r_d, r_ak, ak_ak = [sums[:, n : n + 1] for n in range(6)]
         old_curve = state[1][0:1, 0:1]
         beta = k_img / old_curve
         curve = k_ak - 2.0 * beta * k_img + beta * beta * old_curve
         alpha = (r_k - beta * r_d) / curve
-
-        show = pltpu.make_async_copy(fresh, image_out.at[i], image_s)
-        show.start()
 
         @pl.when(i == 0)
         def _():
@@ -583,7 +586,7 @@
                 res[at] = res[at] - alpha * applied
                 return carry
 
-            lax.fori_loop(0, 16, update, 0)
+            lax.fori_loop(0, 16, update, 0, unroll=4)
 
         steps_out[i] = jnp.broadcast_to(alpha, (8, 128))
         steps_out[2 + i] = jnp.broadcast_to(beta, (8, 128))

time: 120 us -> 115 us (0.958)
  Pallas kernels: 120 us -> 114 us
    pallas_call x1, Pallas kernels: 117 us -> 112 us  [local(): pl.pallas_call(kernel, out_shape=[pair, pair, jax.ShapeDtypeStruct((4, 8,...]
where the time goes in v4:
time: 115 us
  Pallas kernels  114 us (99%)
    pallas_call x1, Pallas kernels, local(): pl.pallas_call(kernel, out_shape=[pair, pair, jax.ShapeDtypeStruct((4, 8,...  112 us
    pallas_call x1, Pallas kernels, local(): pl.pallas_call(last, grid=(LX // 2,), out_shape=[jax.ShapeDtypeStruct(fie...  2.83 us

profile of v4, /device:TPU:1, one launch (start us, length us, event | category | flops | bytes accessed | tf_op | source)
XLA Modules:
  0.0 115.0 jit_solution(12628977927018106896)
XLA Ops:
  0.6 111.5 %shard_map.184 = (f32[2,4,128,256]{3,2,1,0:T(8,128)}, f32[2,4,128,256]{3,2,1,0:T(8,128)}, f32[4,8,128]{2,1,0:T(8,128)}) custom-call(f32[4,128,256]{2,1,0:T(8,128)} %rs.3, bf16[4,128,256]{2,1,0:T(8,128)(2,1)} %perm_in.1, f32[3,16]{1,0:T(4,128)} %bitcast.1, f32[16,17]{1,0:T(8,128)} %mix_in.1, f32[17]{0:T(128)} %pw.1, f32[16,17]{1,0:T(8,128)} %mix_in.1, ...), custom_call_target="tpu_custom_call" | custom-call | tf_op jit(solution)/shard_map/pallas_call | solution.py:664
  112.2 2.8 %shard_map.185 = (f32[4,128,256]{2,1,0:T(8,128)}, f32[4,128,256]{2,1,0:T(8,128)}, f32[2,4,128,256]{3,2,1,0:T(8,128)}) custom-call(f32[4,8,128]{2,1,0:T(8,128)} %get-tuple-element.6.steps, f32[4,128,256]{2,1,0:T(8,128)} %rs.3, f32[2,4,128,256]{3,2,1,0:T(8,128)} %get-tuple-element.7.kept_in, f32[2,4,128,256]{3,2,1,0:T(8,128)} %get-tuple-element.8.image_in), custom_call_target="tpu_custom_call" | custom-call | tf_op jit(solution)/shard_map/pallas_call | solution.py:680

commit v5 on v4

--- a/solution.py
+++ b/solution.py
@@ -214,7 +214,7 @@
 
     for copy in loads[1:5]:
         copy.wait()
-    lax.fori_loop(0, 16, second_pass, 0)
+    lax.fori_loop(0, 16, second_pass, 0, unroll=2)
     mix_high, mix_low = split(mixv[:, 0:CH] * 0.5)
     rows_iota = lax.broadcasted_iota(jnp.int32, (128, 256), 0)
     lane_iota = lax.broadcasted_iota(jnp.int32, (128, 256), 1)
@@ -274,7 +274,7 @@
                 faces[n, x, pl.ds(y, 32), :] = 2.0 * here * other / (here + other)
             return carry
 
-        lax.fori_loop(0, 16, face_pass, 0)
+        lax.fori_loop(0, 16, face_pass, 0, unroll=2)
 
     for copy in loads[5:]:
         copy.wait()
@@ -460,7 +460,7 @@
             padk[x + 1, pl.ds(pl.multiple_of(y + 8, 8), 32), :] = jnp.full((32, NZ), pw[CH], F32)
             return carry
 
-        lax.fori_loop(0, 16, clear, 0)
+        lax.fori_loop(0, 16, clear, 0, unroll=4)
 
         def turn(oq):
             whole = send(
@@ -564,7 +564,7 @@
             )
             return tuple(total + fold8(term) for total, term in zip(totals, terms))
 
-        totals = lax.fori_loop(0, 16, operator_pass, tuple(jnp.zeros((8, NZ), F32) for _ in range(6)), unroll=2)
+        totals = lax.fori_loop(0, 16, operator_pass, tuple(jnp.zeros((8, NZ), F32) for _ in range(6)), unroll=4)
         sums_begin(1 + i, tile_of(totals))
         show = pltpu.make_async_copy(fresh, image_out.at[i], image_s)
         show.start()

time: 115 us -> 115 us (level)
  no operation moved by 1% of the time
where the time goes in v5:
time: 115 us
  Pallas kernels  114 us (99%)
    pallas_call x1, Pallas kernels, local(): pl.pallas_call(kernel, out_shape=[pair, pair, jax.ShapeDtypeStruct((4, 8,...  111 us
    pallas_call x1, Pallas kernels, local(): pl.pallas_call(last, grid=(LX // 2,), out_shape=[jax.ShapeDtypeStruct(fie...  2.83 us

profile of v5, /device:TPU:1, one launch (start us, length us, event | category | flops | bytes accessed | tf_op | source)
XLA Modules:
  0.0 114.6 jit_solution(5254312666627808091)
XLA Ops:
  0.6 111.1 %shard_map.184 = (f32[2,4,128,256]{3,2,1,0:T(8,128)}, f32[2,4,128,256]{3,2,1,0:T(8,128)}, f32[4,8,128]{2,1,0:T(8,128)}) custom-call(f32[4,128,256]{2,1,0:T(8,128)} %rs.3, bf16[4,128,256]{2,1,0:T(8,128)(2,1)} %perm_in.1, f32[3,16]{1,0:T(4,128)} %bitcast.1, f32[16,17]{1,0:T(8,128)} %mix_in.1, f32[17]{0:T(128)} %pw.1, f32[16,17]{1,0:T(8,128)} %mix_in.1, ...), custom_call_target="tpu_custom_call" | custom-call | tf_op jit(solution)/shard_map/pallas_call | solution.py:664
  111.8 2.8 %shard_map.185 = (f32[4,128,256]{2,1,0:T(8,128)}, f32[4,128,256]{2,1,0:T(8,128)}, f32[2,4,128,256]{3,2,1,0:T(8,128)}) custom-call(f32[4,8,128]{2,1,0:T(8,128)} %get-tuple-element.6.steps, f32[4,128,256]{2,1,0:T(8,128)} %rs.3, f32[2,4,128,256]{3,2,1,0:T(8,128)} %get-tuple-element.7.kept_in, f32[2,4,128,256]{3,2,1,0:T(8,128)} %get-tuple-element.8.image_in), custom_call_target="tpu_custom_call" | custom-call | tf_op jit(solution)/shard_map/pallas_call | solution.py:680
